TPU v7x, 32 devices: a whole 2x2x4 slice. The times are simulated.
32 devices in a mesh: row: 8 (over z, core), col: 4 (over y, x).
Axes of the slice: x: 2, y: 2, z: 4, core: 2. Of those that a mesh axis runs over, the one named last changes fastest.
Arguments:
- out_cotangent: bfloat16 [512, 8192], P('row', 'col'), may hold values from -1.75 to 1.75
- saved_input: bfloat16 [512, 8192], P('row', 'col'), may hold values from -6 to 6
- scan_output: bfloat16 [512, 16384], P('col', 'row'), may hold values from -6 to 6
- gate_input: bfloat16 [512, 16384], P('col', 'row'), may hold values from -8 to 8
- branch_grad: bfloat16 [512, 16384], P('col', 'row'), may hold values from -1.75 to 1.75
- out_weight: bfloat16 [16384, 8192], P('row', 'col'), may hold values from -0.046875 to 0.046875
- in_weight: bfloat16 [8192, 2, 16384], P('col', None, 'row'), may hold values from -0.0625 to 0.0625
Outputs:
- input_grad: bfloat16 [512, 8192], P('row', 'col')
- scan_grad: bfloat16 [512, 16384], P('col', 'row')
- in_weight_grad: float32 [8192, 2, 16384], P('col', None, 'row')
- out_weight_grad: float32 [16384, 8192], P('row', 'col')
All inputs are finite; a program needn't handle non-finite values.
Results may differ from a plain program's by a relative error of at most 0.025.
Values may be sent and summed in bfloat16 or wider, within the bound.
No kernel may reach another device: no remote copies, remote signals or barrier semaphores. Data moves between devices by JAX's collectives and lax.ppermute only.
A program may use at most 192 MiB of HBM per device.

v0:
```python
import jax
import jax.numpy as jnp
from jax import lax
from jax.sharding import PartitionSpec as P


def gate_backward(summed, scan_output, gate_input):
    gate_value = gate_input.astype(jnp.float32)
    sigmoid_gate = jax.nn.sigmoid(gate_value)
    silu_gate = gate_value * sigmoid_gate
    scan_value = scan_output.astype(jnp.float32)
    gated = (scan_value * silu_gate).astype(jnp.bfloat16)
    gate_grad = (
        summed * scan_value * sigmoid_gate * (1.0 + gate_value * (1.0 - sigmoid_gate))
    ).astype(jnp.bfloat16)
    scan_grad = (summed * silu_gate).astype(jnp.bfloat16)
    return (gated, gate_grad, scan_grad)


def per_device(
    out_cotangent, saved_input, scan_output, gate_input, branch_grad, out_weight, in_weight
):
    cotangent = lax.all_gather(out_cotangent, "row", axis=0, tiled=True)
    shares = lax.psum_scatter(
        lax.dot_general(
            cotangent, out_weight, (((1,), (1,)), ((), ())), preferred_element_type=jnp.float32
        ).astype(jnp.bfloat16),
        "col",
        scatter_dimension=0,
        tiled=True,
    ).astype(jnp.float32)
    gated, gate_grad, scan_grad = gate_backward(shares, scan_output, gate_input)
    gated_all, branch_all, gate_grad_all = (
        lax.all_gather(gated, "col", axis=0, tiled=True),
        lax.all_gather(branch_grad, "col", axis=0, tiled=True),
        lax.all_gather(gate_grad, "col", axis=0, tiled=True),
    )
    out_weight_grad = lax.dot_general(
        gated_all, cotangent, (((0,), (0,)), ((), ())), preferred_element_type=jnp.float32
    )
    branch_weight = in_weight[:, 0, :]
    gate_weight = in_weight[:, 1, :]
    branch_rows = branch_all
    gate_rows = gate_grad_all
    total = lax.dot_general(
        branch_rows, branch_weight, (((1,), (1,)), ((), ())), preferred_element_type=jnp.float32
    )
    input_grad = lax.psum_scatter(
        (
            total
            + lax.dot_general(
                gate_rows, gate_weight, (((1,), (1,)), ((), ())), preferred_element_type=jnp.float32
            )
        ).astype(jnp.bfloat16),
        "row",
        scatter_dimension=0,
        tiled=True,
    )
    piece = lax.all_gather(saved_input, "row", axis=0, tiled=True)
    branch_rows = branch_all
    gate_rows = gate_grad_all
    branch_sum = lax.dot_general(
        piece, branch_rows, (((0,), (0,)), ((), ())), preferred_element_type=jnp.float32
    )
    gate_sum = lax.dot_general(
        piece, gate_rows, (((0,), (0,)), ((), ())), preferred_element_type=jnp.float32
    )
    in_weight_grad = jnp.stack([branch_sum, gate_sum], axis=1)
    return (input_grad, scan_grad, in_weight_grad, out_weight_grad)


def solution(mesh):
    return jax.shard_map(
        per_device,
        mesh=mesh,
        in_specs=(
            P("row", "col"),
            P("row", "col"),
            P("col", "row"),
            P("col", "row"),
            P("col", "row"),
            P("row", "col"),
            P("col", None, "row"),
        ),
        out_specs=(P("row", "col"), P("col", "row"), P("col", None, "row"), P("row", "col")),
        check_vma=False,
    )
```

profile of v0, /device:TPU:0, one launch (start us, length us, event | category | flops | bytes accessed | tf_op | source)
XLA Modules:
  0.0 299.1 jit_solution(14388666437527571498)
XLA Ops:
  7.2 0.7 all-gather.8.cloned.1.call-update
  7.9 0.0 reduce-scatter.3.cloned.1.call-start
  8.0 33.5 %all-gather.8.cloned.1.call-done = bf16[512,2048]{1,0:T(8,128)(2,1)} async-done(((bf16[64,2048]{1,0:T(8,128)(2,1)}), bf16[512,2048]{1,0:T(8,128)(2,1)}) %all-gather.8.cloned.1.call-update) | async-done | bytes 2097168 | tf_op jit(solution)/shard_map/all_gather | solution.py:23
  41.4 9.9 %convolution_convert_fusion = bf16[512,2048]{1,0:T(8,128)(2,1)} fusion(bf16[512,2048]{1,0:T(8,128)(2,1)} %all-gather.8.cloned.1.call-done, bf16[2048,2048]{1,0:T(8,128)(2,1)} %param.12), kind=kOutput, calls=%fused_computation.8 | convolution fusion | flops 4296015872 | bytes 12582912 | tf_op jit(solution)/shard_map/dot_general | solution.py:25
  51.3 0.0 all-gather.10.cloned.1.call-start
  51.4 34.8 %reduce-scatter.3.cloned.1.call-done = bf16[128,2048]{1,0:T(8,128)(2,1)} async-done(((bf16[512,2048]{1,0:T(8,128)(2,1)}), bf16[128,2048]{1,0:T(8,128)(2,1)}) %reduce-scatter.3.cloned.1.call-update) | async-done | bytes 524304 | tf_op jit(solution)/shard_map/reduce_scatter | solution.py:24
  86.2 2.8 fusion.6
  89.0 0.0 all-gather.6.cloned.1.call-start
  89.0 0.5 all-gather.6.cloned.1.call-update
  89.6 0.0 all-gather.12.cloned.1.call-start
  89.6 0.5 all-gather.12.cloned.1.call-update
  90.2 0.5 all-gather.14.cloned.1.call-update
  90.7 0.0 reduce-scatter.5.cloned.1.call-start
  90.8 32.9 %fusion.11 = (bf16[2048,1,2048]{2,1,0:T(2,128)(2,1)}, bf16[2048,1,2048]{2,1,0:T(2,128)(2,1)}) fusion(bf16[2048,2,2048]{2,1,0:T(2,128)(2,1)} %param.13), kind=kLoop, calls=%fused_computation.24 | loop fusion | bytes 33554432 | tf_op jit(solution)/shard_map/slice | solution.py:41
  123.7 0.8 all-gather.10.cloned.1.call-done
  124.5 14.0 %fusion = f32[512,2048]{1,0:T(8,128)} fusion(bf16[512,2048]{1,0:T(8,128)(2,1)} %all-gather.10.cloned.1.call-done, bf16[2048,1,2048]{2,1,0:T(2,128)(2,1)} %get-tuple-element.13), kind=kOutput, calls=%fused_computation.4 | convolution fusion | flops 4294967296 | bytes 14680064 | tf_op jit(solution)/shard_map/dot_general | solution.py:51
  138.5 23.2 %all-gather.6.cloned.1.call-done = bf16[512,2048]{1,0:T(8,128)(2,1)} async-done(((bf16[128,2048]{1,0:T(8,128)(2,1)}), bf16[512,2048]{1,0:T(8,128)(2,1)}) %all-gather.6.cloned.1.call-update) | async-done | bytes 2097168 | tf_op jit(solution)/shard_map/all_gather | solution.py:35
  161.7 14.7 %add_convert_fusion = bf16[512,2048]{1,0:T(8,128)(2,1)} fusion(f32[512,2048]{1,0:T(8,128)} %fusion, bf16[512,2048]{1,0:T(8,128)(2,1)} %all-gather.6.cloned.1.call-done, bf16[2048,1,2048]{2,1,0:T(2,128)(2,1)} %get-tuple-element.12), kind=kOutput, calls=%fused_computation.7 | convolution fusion | flops 4297064448 | bytes 16777216 | tf_op jit(solution)/shard_map/dot_general | solution.py:45
  176.4 16.0 %all-gather.12.cloned.1.call-done = bf16[512,2048]{1,0:T(8,128)(2,1)} async-done(((bf16[64,2048]{1,0:T(8,128)(2,1)}), bf16[512,2048]{1,0:T(8,128)(2,1)}) %all-gather.12.cloned.1.call-update) | async-done | bytes 2097168 | tf_op jit(solution)/shard_map/all_gather | solution.py:59
  192.3 7.3 %convolution_bitcast_fusion.1 = f32[2048,1,2048]{2,0,1:T(8,128)S(1)} fusion(bf16[512,2048]{1,0:T(8,128)(2,1)} %all-gather.12.cloned.1.call-done, bf16[512,2048]{1,0:T(8,128)(2,1)} %all-gather.6.cloned.1.call-done), kind=kOutput, calls=%fused_computation.2 | convolution fusion | flops 4294967296 | bytes 20971520 | tf_op jit(solution)/shard_map/dot_general | solution.py:62
  199.7 8.6 %convolution_bitcast_fusion = f32[2048,1,2048]{2,0,1:T(8,128)} fusion(bf16[512,2048]{1,0:T(8,128)(2,1)S(1)} %copy-done.3, bf16[512,2048]{1,0:T(8,128)(2,1)S(1)} %copy-done.4), kind=kOutput, calls=%fused_computation.1 | convolution fusion | flops 4294967296 | bytes 20971520 | tf_op jit(solution)/shard_map/dot_general | solution.py:65
  208.3 18.6 %pad_maximum_fusion = f32[2048,2,2048]{2,0,1:T(8,128)} fusion(f32[2048,1,2048]{2,0,1:T(8,128)} %convolution_bitcast_fusion, f32[2048,1,2048]{2,0,1:T(8,128)S(1)} %convolution_bitcast_fusion.1), kind=kLoop, calls=%fused_computation | loop fusion | flops 8388608 | bytes 67108864 | tf_op jit(solution)/shard_map/stack | solution.py:68
  226.9 55.2 %copy.16 = f32[2048,2,2048]{2,1,0:T(2,128)} copy(f32[2048,2,2048]{2,0,1:T(8,128)} %pad_maximum_fusion) | data formatting | bytes 67108864
  282.1 10.1 %fusion.12 = f32[2048,2048]{1,0:T(8,128)} fusion(bf16[512,2048]{1,0:T(8,128)(2,1)} %all-gather.14.cloned.1.call-done, bf16[512,2048]{1,0:T(8,128)(2,1)S(1)} %copy-done.2), kind=kOutput, calls=%fused_computation.25 | convolution fusion | flops 4294967296 | bytes 20971520 | tf_op jit(solution)/shard_map/dot_general | solution.py:38
  (17 shorter events, 0.1 us)
Async XLA Ops:
  7.2 34.3 %all-gather.8.cloned.1.call-start = ((), (), s32[]{:S(2)}) async-start(), calls=%async_computation.3 | async-start | bytes 2359296 | tf_op jit(solution)/shard_map/all_gather | solution.py:23
  7.9 78.3 %copy-start = (bf16[128,2048]{1,0:T(8,128)(2,1)S(1)}, bf16[128,2048]{1,0:T(8,128)(2,1)}, u32[]{:S(2)}) copy-start(bf16[128,2048]{1,0:T(8,128)(2,1)} %param.9) | copy-start | bytes 1572868
  7.9 78.3 %copy-start.1 = (bf16[128,2048]{1,0:T(8,128)(2,1)S(1)}, bf16[128,2048]{1,0:T(8,128)(2,1)}, u32[]{:S(2)}) copy-start(bf16[128,2048]{1,0:T(8,128)(2,1)} %param.10) | copy-start | bytes 1572868
  7.9 78.3 %reduce-scatter.3.cloned.1.call-start = ((), (), s32[]{:S(2)}) async-start(), calls=%async_computation.4 | async-start | bytes 2621440 | tf_op jit(solution)/shard_map/reduce_scatter | solution.py:24
  51.3 73.2 %all-gather.10.cloned.1.call-start = ((), (), s32[]{:S(2)}) async-start(), calls=%async_computation.5 | async-start | bytes 2621440 | tf_op jit(solution)/shard_map/all_gather | solution.py:36
  89.0 72.7 %all-gather.6.cloned.1.call-start = ((), (), s32[]{:S(2)}) async-start(), calls=%async_computation.2 | async-start | bytes 2621440 | tf_op jit(solution)/shard_map/all_gather | solution.py:35
  89.6 102.8 %all-gather.12.cloned.1.call-start = ((), (), s32[]{:S(2)}) async-start(), calls=%async_computation.7 | async-start | bytes 2359296 | tf_op jit(solution)/shard_map/all_gather | solution.py:59
  90.2 191.9 %all-gather.14.cloned.1.call-start = ((), (), s32[]{:S(2)}) async-start(), calls=%async_computation.8 | async-start | bytes 2621440 | tf_op jit(solution)/shard_map/all_gather | solution.py:34
  90.7 201.5 %reduce-scatter.5.cloned.1.call-start = ((), (), s32[]{:S(2)}) async-start(), calls=%async_computation.6 | async-start | bytes 2359296 | tf_op jit(solution)/shard_map/reduce_scatter | solution.py:48
  176.3 23.3 %copy-start.3 = (bf16[512,2048]{1,0:T(8,128)(2,1)S(1)}, bf16[512,2048]{1,0:T(8,128)(2,1)}, u32[]{:S(2)}) copy-start(bf16[512,2048]{1,0:T(8,128)(2,1)} %all-gather.10.cloned.1.call-done) | copy-start | bytes 6291460
  192.3 7.3 %copy-start.4 = (bf16[512,2048]{1,0:T(8,128)(2,1)S(1)}, bf16[512,2048]{1,0:T(8,128)(2,1)}, u32[]{:S(2)}) copy-start(bf16[512,2048]{1,0:T(8,128)(2,1)} %all-gather.12.cloned.1.call-done) | copy-start | bytes 6291460
  226.9 55.2 %copy-start.2 = (bf16[512,2048]{1,0:T(8,128)(2,1)S(1)}, bf16[512,2048]{1,0:T(8,128)(2,1)}, u32[]{:S(2)}) copy-start(bf16[512,2048]{1,0:T(8,128)(2,1)} %all-gather.8.cloned.1.call-done) | copy-start | bytes 6291460
Sparse Core Ops, SparseCore 0:
  9.6 31.7 all-gather.7
  51.4 34.6 reduce-scatter.2
  89.1 35.3 all-gather.9
  126.3 35.2 all-gather.5
  163.2 29.0 all-gather.11
  194.2 34.7 all-gather.13
  232.0 35.7 reduce-scatter.4
where the time goes:
time: 299 us
  waiting for transfers between devices  111 us (37%)
  local copies, waits for them, and re-layouts  88.1 us (29%)
  matrix products  64.6 us (22%)
  other arithmetic  21.4 us (7%)
  between operations  14.2 us (5%)
    unnamed x11, local copies, waits for them, and re-layouts  55.2 us
    reduce_scatter x1, waiting for transfers between devices, per_device(): lax.psum_scatter(lax.dot_general(cotangent, out_weight, (((1,), (1,)), ((...  34.8 us
    all_gather x1, waiting for transfers between devices, per_device(): cotangent = lax.all_gather(out_cotangent, 'row', axis=0, tiled=True)  33.5 us
    slice x1, local copies, waits for them, and re-layouts, per_device(): branch_weight = in_weight[:, 0, :]  32.9 us
    all_gather x1, waiting for transfers between devices, per_device(): lax.all_gather(branch_grad, 'col', axis=0, tiled=True)  23.2 us
    another operation x1, other arithmetic, per_device(): in_weight_grad = jnp.stack([branch_sum, gate_sum], axis=1)  18.6 us
    all_gather x1, waiting for transfers between devices, per_device(): piece = lax.all_gather(saved_input, 'row', axis=0, tiled=True)  16 us
    dot_general x1, matrix products, per_device(): lax.dot_general(branch_rows, branch_weight, (((1,), (1,)), ((), ())), pre...  14.7 us
  transfers between devices with their start and end apart: 7, of which 5 were waited for; matrix products, arithmetic and copies ran while one was open for 54% of the time, Pallas kernels for 0%

commit v1 on v0

v1 whole, which is shorter than its diff:
```python
import functools

import jax
import jax.numpy as jnp
from jax import lax
from jax.experimental import pallas as pl
from jax.experimental.pallas import tpu as pltpu
from jax.sharding import PartitionSpec as P

BF16 = jnp.bfloat16
F32 = jnp.float32
MIB = 2**20
WEIGHT = 8
LANES = 128
PARTNERS = (1, 2, 3)
COLUMN, CORE, CHIP = 0, 1, 2


def run(body, where, args, in_specs, outs, out_specs, grid, scratch=(), flops=0, moved=0, vmem=16, aliases=None):
    return pl.pallas_call(
        body,
        out_shape=outs,
        grid_spec=pltpu.PrefetchScalarGridSpec(
            num_scalar_prefetch=1,
            grid=grid,
            in_specs=in_specs,
            out_specs=out_specs,
            scratch_shapes=list(scratch),
        ),
        input_output_aliases=aliases or {},
        cost_estimate=pl.CostEstimate(flops=flops, bytes_accessed=moved, transcendentals=0),
        compiler_params=pltpu.CompilerParams(vmem_limit_bytes=vmem * MIB),
    )(where, *args)


def far(pieces):
    return [pl.BlockSpec(memory_space=pl.ANY) for _ in pieces]


def lay(moves, sems, groups=1):
    first = pl.program_id(0) == 0
    copies = [pltpu.make_async_copy(piece, place, sems.at[index]) for index, (piece, place) in enumerate(moves)]
    size = len(copies) // groups

    @pl.when(first)
    def _():
        for copy in copies:
            copy.start()

    def arrived(group):
        @pl.when(first)
        def _():
            for copy in copies[group * size : (group + 1) * size]:
                copy.wait()

    return arrived


DEPTH = 3
PARTS = 4


def stream(source, buffer, sems):
    step, steps = pl.program_id(0), pl.num_programs(0)
    rows = buffer.shape[1] // PARTS

    def copies(step):
        slot = lax.rem(step, DEPTH)
        for part in range(PARTS):
            here = pl.ds(part * rows, rows)
            yield pltpu.make_async_copy(source(step).at[here], buffer.at[slot, here], sems.at[slot, part])

    @pl.when(step == 0)
    def _():
        for ahead in range(DEPTH - 1):
            for copy in copies(ahead):
                copy.start()

    @pl.when(step + DEPTH - 1 < steps)
    def _():
        for copy in copies(step + DEPTH - 1):
            copy.start()

    for copy in copies(step):
        copy.wait()
    return buffer.at[lax.rem(step, DEPTH)]


def streamed(shape, kind):
    return [pltpu.VMEM((DEPTH, *shape), kind), pltpu.SemaphoreType.DMA((DEPTH, PARTS))]


HBM = pl.BlockSpec(memory_space=pltpu.HBM)


def stay(value):
    return pltpu.with_memory_space_constraint(value, pltpu.HBM)


def at(start, size):
    return pl.ds(pl.multiple_of(start, size), size)


def dot_nt(rows, weight):
    return lax.dot_general(rows, weight, (((1,), (1,)), ((), ())), preferred_element_type=F32)


def dot_turned(rows, weight):
    return dot_nt(weight, rows).T


def dot_nn(rows, weight):
    return lax.dot_general(rows, weight, (((1,), (0,)), ((), ())), preferred_element_type=F32)


def split_body(where, source, branch, gate, order, *buffers):
    lines = buffers[0].shape[1]
    packed = stream(lambda step: source.at[at(step * lines, lines)], *buffers)

    @pl.when(pl.program_id(0) == 0)
    def _():
        row = lax.broadcasted_iota(jnp.int32, (256, 256), 0)
        column = lax.broadcasted_iota(jnp.int32, (256, 256), 1)
        source = (row & 7) * 32 + ((row >> 3) & 15) * 2 + (row >> 7)
        order[...] = jnp.where(column == source, 1.0, 0.0).astype(BF16)

    for group in range(branch.shape[0] // 16):
        low, high = (packed[pl.ds((2 * group + part) * 256, 256), :] for part in range(2))
        moved = dot_nn(order[...], jnp.concatenate([low, high], axis=1))
        parts = [moved[:, part * LANES : (part + 1) * LANES].reshape(2, 16, 1, 8, LANES) for part in range(2)]
        rows = jnp.concatenate(parts, axis=2).reshape(2, 16, 16, LANES).astype(BF16)
        for half, out in enumerate((branch, gate)):
            for tile in range(16):
                out[pl.ds(group * 16, 16), tile * LANES : (tile + 1) * LANES] = rows[half, tile]


def split_weight(where, in_weight):
    features, _, channels = in_weight.shape
    packed = (
        in_weight.reshape(features, 2, channels // LANES, LANES)
        .transpose(0, 2, 1, 3)
        .reshape(features * 2 * channels // LANES, LANES)
    )
    block = 128
    out = pltpu.HBM((features, channels), BF16)
    out_spec = pl.BlockSpec((block, channels), lambda i, *_: (i, 0))
    return run(
        split_body,
        where,
        (stay(packed),),
        [HBM],
        [out, out],
        [out_spec, out_spec],
        (features // block,),
        scratch=[pltpu.VMEM((256, 256), BF16), *streamed((block * 2 * channels // LANES, LANES), BF16)],
        flops=WEIGHT * 512 * 2 * features * channels,
        moved=WEIGHT * 8 * features * channels,
    )


def share_body(where, *refs):
    pieces, source, own, sends, rows, sems, buffers = refs[:4], refs[4], refs[5], refs[6:9], *refs[9:11], refs[11:]
    block = buffers[0].shape[1]
    weight = stream(lambda step: source.at[at(step * block, block)], *buffers)
    first = where[COLUMN] ^ where[CHIP]
    lay([(piece, rows.at[at((first ^ index) * 64, 64)]) for index, piece in enumerate(pieces)], sems)(0)

    total = dot_turned(rows[...], weight[...])
    own[...] = total[:64]
    for index, send in enumerate(sends):
        send[...] = total[(index + 1) * 64 : (index + 2) * 64].astype(BF16)


def share(where, pieces, weight):
    channels, features = weight.shape
    block = 512
    spec = pl.BlockSpec((64, block), lambda i, *_: (0, i))
    own, send = jax.ShapeDtypeStruct((64, channels), F32), pltpu.HBM((64, channels), BF16)
    return run(
        share_body,
        where,
        (*pieces, stay(weight)),
        far(pieces) + [HBM],
        [own, send, send, send],
        [spec] * 4,
        (channels // block,),
        scratch=[
            pltpu.VMEM((256, features), BF16),
            pltpu.SemaphoreType.DMA((4,)),
            *streamed((block, features), BF16),
        ],
        flops=2 * 256 * channels * features // WEIGHT,
        moved=2 * channels * features // WEIGHT,
    )


def gate_body(where, own, *refs):
    received, scan, gate = refs[:3], refs[3], refs[4]
    gate_grad, scan_grad = refs[-2:]
    summed = own[...]
    for term in received:
        summed = summed + term[...].astype(F32)
    value = gate[...].astype(F32)
    sigmoid = jax.nn.sigmoid(value)
    scan_value = scan[...].astype(F32)
    gate_grad[...] = (summed * scan_value * sigmoid * (1.0 + value * (1.0 - sigmoid))).astype(BF16)
    scan_grad[...] = (summed * (value * sigmoid)).astype(BF16)


def gate_step(where, own, received, scan, gate, previous):
    channels = scan.shape[1]
    block = 512
    spec = pl.BlockSpec((64, block), lambda i, *_: (0, i))
    mine = pl.BlockSpec((64, block), lambda i, where: (where[CORE], i))
    args = [own, *received, scan, gate]
    specs = [spec] * 4 + [mine, mine]
    aliases = {}
    if previous is not None:
        args.append(previous)
        specs.append(pl.BlockSpec(memory_space=pl.ANY))
        aliases = {7: 1}
    return run(
        gate_body,
        where,
        args,
        specs,
        [jax.ShapeDtypeStruct((64, channels), BF16), jax.ShapeDtypeStruct(scan.shape, BF16)],
        [spec, mine],
        (channels // block,),
        flops=WEIGHT * 64 * channels * 16,
        moved=WEIGHT * 64 * channels * 16,
        aliases=aliases,
    )


def branch_body(where, *refs):
    branch, source, mine, other, rows, sems, *buffers = refs
    block = buffers[0].shape[1]
    weight = stream(lambda step: source.at[at(step * block, block)], *buffers)
    core = where[CORE]
    moves = []
    for index in range(4):
        start = (where[CHIP] ^ index) * 128
        moves.append((branch.at[at(start + core * 64, 64)], rows.at[pl.ds(index * 64, 64)]))
        moves.append((branch.at[at(start + (1 - core) * 64, 64)], rows.at[pl.ds(256 + index * 64, 64)]))
    lay(moves, sems)(0)
    total = dot_nt(rows[...], weight[...])
    mine[...] = total[:256].reshape(mine.shape)
    other[...] = total[256:].reshape(other.shape).astype(BF16)


def branch_part(where, branch, weight):
    features, channels = weight.shape
    block = 512
    spec = pl.BlockSpec((4, 64, block), lambda i, *_: (0, 0, i))
    return run(
        branch_body,
        where,
        (branch, stay(weight)),
        [pl.BlockSpec(memory_space=pl.ANY), HBM],
        [pltpu.HBM((4, 64, features), F32), pltpu.HBM((4, 64, features), BF16)],
        [spec, spec],
        (features // block,),
        scratch=[
            pltpu.VMEM((512, channels), BF16),
            pltpu.SemaphoreType.DMA((8,)),
            *streamed((block, channels), BF16),
        ],
        flops=2 * 512 * channels * features // WEIGHT,
        moved=2 * channels * features // WEIGHT,
    )


def input_body(where, *refs):
    pieces, source, branch, out, rows, sems, buffers = refs[:4], *refs[4:9], refs[9:]
    block = buffers[0].shape[1]
    weight = stream(lambda step: source.at[at(step * block, block)], *buffers)
    first = where[COLUMN] ^ where[CHIP]
    lay([(piece, rows.at[at((first ^ index) * 64, 64)]) for index, piece in enumerate(pieces)], sems)(0)
    total = dot_turned(rows[...], weight[...])
    out[...] = (total.reshape(out.shape) + branch[...].astype(F32)).astype(out.dtype)


def input_part(where, pieces, weight, branch):
    features, channels = weight.shape
    block = 512
    spec = pl.BlockSpec((4, 64, block), lambda i, *_: (0, 0, i))
    return run(
        input_body,
        where,
        (*pieces, stay(weight), stay(branch)),
        far(pieces) + [HBM, spec],
        jax.ShapeDtypeStruct((4, 64, features), branch.dtype),
        spec,
        (features // block,),
        scratch=[
            pltpu.VMEM((256, channels), BF16),
            pltpu.SemaphoreType.DMA((4,)),
            *streamed((block, channels), BF16),
        ],
        flops=WEIGHT * 2 * 256 * channels * features,
        moved=WEIGHT * 2 * channels * features,
    )


def combine_body(where, here, there, *outs):
    for index, out in enumerate(outs):
        out[...] = (here[index] + there[index].astype(F32)).astype(out.dtype)


def combine(where, here, there):
    features = here.shape[2]
    block = 512
    four = pl.BlockSpec((4, 64, block), lambda i, *_: (0, 0, i))
    one = pl.BlockSpec((64, block), lambda i, *_: (0, i))
    return run(
        combine_body,
        where,
        (here, there),
        [four, four],
        [pltpu.HBM((64, features), F32)] + [jax.ShapeDtypeStruct((64, features), BF16)] * 3,
        [one] * 4,
        (features // block,),
        flops=256 * features,
        moved=256 * features * 9,
    )


def in_grad_body(block, tiles, where, *refs):
    branch, mine, other, saved, out, rows, order, held, sems, out_sems = refs[0], refs[1:5], refs[5:9], *refs[9:]
    step, steps = pl.program_id(0), pl.num_programs(0)
    slot = lax.rem(step, 2)
    group, lines = block // 8, 2 * tiles
    pitch = group * lines + 1
    moves = [(branch.at[pl.ds(start, 64)], rows.at[0, pl.ds(start, 64)]) for start in range(0, 512, 64)]
    for index in range(4):
        start = (where[COLUMN] ^ index) * 128
        moves.append((mine[index], rows.at[1, at(start + where[CORE] * 64, 64)]))
        moves.append((other[index], rows.at[1, at(start + (1 - where[CORE]) * 64, 64)]))
    arrived = lay(moves, sems, 2)

    @pl.when(step == 0)
    def _():
        row = lax.broadcasted_iota(jnp.int32, (block, block), 0)
        column = lax.broadcasted_iota(jnp.int32, (block, block), 1)
        order[...] = jnp.where(column == (row & 7) * group + (row >> 3), 1.0, 0.0).astype(BF16)

    def copy(step, slot, part):
        return pltpu.make_async_copy(
            held.at[slot, pl.ds(part * pitch, group * lines)],
            out.at[pl.ds(pl.multiple_of((step * 8 + part) * group * lines, 8), group * lines)],
            out_sems.at[slot, part],
        )

    @pl.when(step >= 2)
    def _():
        for part in range(8):
            copy(step - 2, slot, part).wait()

    left = dot_nt(order[...], saved[...]).astype(BF16)
    width = 256
    for half in range(2):
        arrived(half)
        for first in range(0, tiles * LANES, width):
            total = dot_nn(left, rows[half, :, first : first + width])
            for tile in range(width // LANES):
                line = 2 * (first // LANES + tile) + half
                for index in range(group):
                    held[slot, pl.ds(index * lines + line, 8, stride=pitch), :] = total[
                        index * 8 : (index + 1) * 8, tile * LANES : (tile + 1) * LANES
                    ]
    for part in range(8):
        copy(step, slot, part).start()

    @pl.when(step == steps - 1)
    def _():
        for part in range(8):
            copy(step - 1, 1 - slot, part).wait()
        for part in range(8):
            copy(step, slot, part).wait()


def in_grad(where, branch, mine, other, saved):
    tokens, features = saved.shape
    channels = mine[0].shape[1]
    tiles = channels // LANES
    block = 256
    pieces = (branch, *mine, *other)
    held = -(-(block * 2 * tiles + 8) // 8) * 8
    out = run(
        functools.partial(in_grad_body, block, tiles),
        where,
        (*map(stay, pieces), stay(saved)),
        far(pieces) + [pl.BlockSpec((tokens, block), lambda i, *_: (0, i))],
        jax.ShapeDtypeStruct((features * 2 * tiles, LANES), F32),
        pl.BlockSpec(memory_space=pl.ANY),
        (features // block,),
        scratch=[
            pltpu.VMEM((2, tokens, channels), BF16),
            pltpu.VMEM((block, block), BF16),
            pltpu.VMEM((2, held, LANES), F32),
            pltpu.SemaphoreType.DMA((16,)),
            pltpu.SemaphoreType.DMA((2, 8)),
        ],
        flops=4 * tokens * features * channels,
        moved=8 * features * channels + 2 * tokens * (features + 2 * channels),
        vmem=32,
    )
    return out.reshape(features, tiles, 2, LANES).transpose(0, 2, 1, 3).reshape(features, 2, channels)


def out_grad_body(where, *refs):
    mine, other, gated, out, right, same, held, sems, out_sems = refs[:4], refs[4:8], *refs[8:]
    step, steps = pl.program_id(0), pl.num_programs(0)
    slot = lax.rem(step, 2)
    _, columns, block, width = held.shape
    moves = []
    for index in range(4):
        start = (where[CHIP] ^ index) * 128
        moves.append((mine[index], right.at[at(start + where[CORE] * 64, 64)]))
        moves.append((other[index], right.at[at(start + (1 - where[CORE]) * 64, 64)]))
    arrived = lay(moves, sems)

    @pl.when(step == 0)
    def _():
        row = lax.broadcasted_iota(jnp.int32, (block, block), 0)
        column = lax.broadcasted_iota(jnp.int32, (block, block), 1)
        same[...] = jnp.where(row == column, 1.0, 0.0).astype(BF16)

    def copy(step, slot, part):
        return pltpu.make_async_copy(
            held.at[slot, part],
            out.at[at(step * block, block), pl.ds(part * width, width)],
            out_sems.at[slot, part],
        )

    rows = dot_nt(same[...], gated[...]).astype(BF16)
    arrived(0)
    for part in range(columns):

        @pl.when(step >= 2)
        def _():
            copy(step - 2, slot, part).wait()

        held[slot, part] = dot_nn(rows, right[:, part * width : (part + 1) * width])
        copy(step, slot, part).start()

    @pl.when(step == steps - 1)
    def _():
        for part in range(columns):
            copy(step - 1, 1 - slot, part).wait()
        for part in range(columns):
            copy(step, slot, part).wait()


def out_grad(where, gated, mine, other):
    tokens, channels = gated.shape
    features = mine[0].shape[1]
    block, width = 512, 512
    pieces = (*mine, *other)
    return run(
        out_grad_body,
        where,
        tuple(map(stay, (*pieces, gated))),
        far(pieces) + [pl.BlockSpec((tokens, block), lambda i, *_: (0, i))],
        jax.ShapeDtypeStruct((channels, features), F32),
        pl.BlockSpec(memory_space=pl.ANY),
        (channels // block,),
        scratch=[
            pltpu.VMEM((tokens, features), BF16),
            pltpu.VMEM((block, block), BF16),
            pltpu.VMEM((2, features // width, block, width), F32),
            pltpu.SemaphoreType.DMA((8,)),
            pltpu.SemaphoreType.DMA((2, features // width)),
        ],
        flops=2 * tokens * channels * features,
        moved=4 * channels * features + 2 * tokens * (channels + features),
        vmem=24,
    )


def to_plane(value, partner):
    return lax.ppermute(value, "col", [(index, index ^ partner) for index in range(4)])


def to_chip(value, partner):
    return lax.ppermute(value, "row", [(index, index ^ (2 * partner)) for index in range(8)])


def to_other_core(value):
    return lax.ppermute(value, "row", [(index, index ^ 1) for index in range(8)])


def after(value, *earlier):
    return lax.optimization_barrier((value, *earlier))[0]


def plane_per_device(
    out_cotangent, saved_input, scan_output, gate_input, branch_grad, out_weight, in_weight
):
    column, row = lax.axis_index("col"), lax.axis_index("row")
    core, chip = row % 2, row // 2
    mine = jnp.stack([column, core, chip]).astype(jnp.int32)
    other = jnp.stack([column, 1 - core, chip]).astype(jnp.int32)

    beside = to_other_core(out_cotangent)
    branch = lax.all_gather(branch_grad, "col", axis=0, tiled=True)
    gate_value = gate_input.astype(F32)
    gated = (scan_output.astype(F32) * (gate_value * jax.nn.sigmoid(gate_value))).astype(BF16)
    branch_weight, gate_weight = split_weight(mine, after(in_weight, beside, gated))
    cot_other = (beside, *(to_chip(beside, partner) for partner in PARTNERS))
    cot_mine = (out_cotangent, *(to_other_core(after(block, branch_weight)) for block in cot_other[1:]))

    share_other = share(other, cot_other, after(out_weight, branch_weight))
    share_mine = share(mine, after(cot_mine, share_other[0]), out_weight)
    saved = lax.all_gather(after(saved_input, share_other[0]), "row", axis=0, tiled=True)
    sums_other = [to_plane(send, partner) for send, partner in zip(share_other[1:], PARTNERS)]
    sums_mine = [to_plane(send, partner) for send, partner in zip(share_mine[1:], PARTNERS)]
    own = after(share_other[0], share_mine[0], branch)
    grad_other, scan_grad = gate_step(other, own, sums_other, scan_output, gate_input, None)
    grad_other = (grad_other, *(to_plane(grad_other, partner) for partner in PARTNERS))
    branch_mine, branch_other = branch_part(mine, after(branch, grad_other[0], sums_mine[0]), branch_weight)
    own = after(share_mine[0], branch_mine)
    grad_mine, scan_grad = gate_step(mine, own, sums_mine, scan_output, gate_input, scan_grad)
    grad_mine = (grad_mine, *(to_plane(grad_mine, partner) for partner in PARTNERS))

    there = input_part(other, grad_other, after(gate_weight, saved), branch_other)
    here = input_part(mine, grad_mine, gate_weight, branch_mine)
    total, *sends = combine(mine, here, to_other_core(there))
    terms = [to_chip(send, partner) for send, partner in zip(sends, PARTNERS)]

    gated = lax.all_gather(after(gated, there), "col", axis=0, tiled=True)
    in_weight_grad = in_grad(mine, branch, grad_mine, grad_other, after(saved, total))
    in_weight_grad, total = lax.optimization_barrier((in_weight_grad, total))
    out_weight_grad = out_grad(mine, gated, after(cot_mine, total), cot_other)
    for term in terms:
        total = total + term.astype(F32)
    return (total.astype(BF16), scan_grad, in_weight_grad, out_weight_grad)


def gate_backward(summed, scan_output, gate_input):
    gate_value = gate_input.astype(jnp.float32)
    sigmoid_gate = jax.nn.sigmoid(gate_value)
    silu_gate = gate_value * sigmoid_gate
    scan_value = scan_output.astype(jnp.float32)
    gated = (scan_value * silu_gate).astype(jnp.bfloat16)
    gate_grad = (
        summed * scan_value * sigmoid_gate * (1.0 + gate_value * (1.0 - sigmoid_gate))
    ).astype(jnp.bfloat16)
    scan_grad = (summed * silu_gate).astype(jnp.bfloat16)
    return (gated, gate_grad, scan_grad)


def per_device(
    out_cotangent, saved_input, scan_output, gate_input, branch_grad, out_weight, in_weight
):
    cotangent = lax.all_gather(out_cotangent, "row", axis=0, tiled=True)
    shares = lax.psum_scatter(
        lax.dot_general(
            cotangent, out_weight, (((1,), (1,)), ((), ())), preferred_element_type=jnp.float32
        ).astype(jnp.bfloat16),
        "col",
        scatter_dimension=0,
        tiled=True,
    ).astype(jnp.float32)
    gated, gate_grad, scan_grad = gate_backward(shares, scan_output, gate_input)
    gated_all, branch_all, gate_grad_all = (
        lax.all_gather(gated, "col", axis=0, tiled=True),
        lax.all_gather(branch_grad, "col", axis=0, tiled=True),
        lax.all_gather(gate_grad, "col", axis=0, tiled=True),
    )
    out_weight_grad = lax.dot_general(
        gated_all, cotangent, (((0,), (0,)), ((), ())), preferred_element_type=jnp.float32
    )
    total = lax.dot_general(
        branch_all, in_weight[:, 0, :], (((1,), (1,)), ((), ())), preferred_element_type=jnp.float32
    ) + lax.dot_general(
        gate_grad_all, in_weight[:, 1, :], (((1,), (1,)), ((), ())), preferred_element_type=jnp.float32
    )
    input_grad = lax.psum_scatter(
        total.astype(jnp.bfloat16), "row", scatter_dimension=0, tiled=True
    )
    piece = lax.all_gather(saved_input, "row", axis=0, tiled=True)
    in_weight_grad = jnp.stack(
        [
            lax.dot_general(piece, grad, (((0,), (0,)), ((), ())), preferred_element_type=jnp.float32)
            for grad in (branch_all, gate_grad_all)
        ],
        axis=1,
    )
    return (input_grad, scan_grad, in_weight_grad, out_weight_grad)


def solution(mesh):
    rows, columns = mesh.shape["row"], mesh.shape["col"]
    body = plane_per_device if (rows, columns) == (8, 4) else per_device
    return jax.shard_map(
        body,
        mesh=mesh,
        in_specs=(
            P("row", "col"),
            P("row", "col"),
            P("col", "row"),
            P("col", "row"),
            P("col", "row"),
            P("row", "col"),
            P("col", None, "row"),
        ),
        out_specs=(P("row", "col"), P("col", "row"), P("col", None, "row"), P("row", "col")),
        check_vma=False,
    )
```

time: 299 us -> 152 us (0.51)
  waiting for transfers between devices: 111 us -> 11.5 us
  Pallas kernels: 0 us -> 93.1 us
  local copies, waits for them, and re-layouts: 88.1 us -> 4.17 us
  matrix products: 64.6 us -> 0 us
  starting transfers between devices: 0.27 us -> 25.1 us
  other arithmetic: 21.4 us -> 3.29 us
    pallas_call x0 -> x11, Pallas kernels: none -> 93.1 us  [run(): pl.pallas_call(body, out_shape=outs, grid_spec=pltpu.PrefetchScalarGridSp...]
    all_gather x5 -> x3, waiting for transfers between devices: 73.4 us -> 0.01 us  [the longest x1 0.01 us: plane_per_device(): branch = lax.all_gather(branch_grad, 'col', axis=0, tiled=True)]
    dot_general x6 -> x0, matrix products: 64.6 us -> none  [the longest x1 14.7 us: per_device(): lax.dot_general(branch_rows, branch_weight, (((1,), (1,)), ((), ())), pre...]
    unnamed x11 -> x48, local copies, waits for them, and re-layouts: 55.2 us -> 4.17 us
    reduce_scatter x2 -> x0, waiting for transfers between devices: 34.8 us -> none  [the longest x1 34.8 us: per_device(): lax.psum_scatter(lax.dot_general(cotangent, out_weight, (((1,), (1,)), ((...]
    slice x1 -> x0, local copies, waits for them, and re-layouts: 32.9 us -> none  [per_device(): branch_weight = in_weight[:, 0, :]]
    ppermute x0 -> x23, starting transfers between devices: none -> 25 us  [the longest x12 14.1 us: to_plane(): lax.ppermute(value, 'col', [(index, index ^ partner) for index in range(4)])]
    another operation x1 -> x2, other arithmetic: 18.6 us -> 0.15 us  [the longest x1 0.08 us: plane_per_device(): other = jnp.stack([column, 1 - core, chip]).astype(jnp.int32)]
  transfers between devices with their start and end apart: 7 -> 26, of which waited for: 5 -> 4; matrix products, arithmetic and copies ran while one was open for 54% -> 2% of each run, Pallas kernels for 0% -> 53%
where the time goes in v1:
time: 152 us; the launch traced here: 151 us
  Pallas kernels  93.1 us (61%)
  starting transfers between devices  25.1 us (17%)
  between operations  14.1 us (9%)
  waiting for transfers between devices  11.5 us (8%)
  local copies, waits for them, and re-layouts  4.17 us (3%)
  other arithmetic  3.29 us (2%)
    pallas_call x11, Pallas kernels, run(): pl.pallas_call(body, out_shape=outs, grid_spec=pltpu.PrefetchScalarGridSp...  93.1 us
    ppermute x12, starting transfers between devices, to_plane(): lax.ppermute(value, 'col', [(index, index ^ partner) for index in range(4)])  14.1 us
    ppermute x6, starting transfers between devices, to_chip(): lax.ppermute(value, 'row', [(index, index ^ 2 * partner) for index in ran...  9.67 us
    ppermute x6, waiting for transfers between devices, to_chip(): lax.ppermute(value, 'row', [(index, index ^ 2 * partner) for index in ran...  7.35 us
    unnamed x48, local copies, waits for them, and re-layouts  4.17 us
    ppermute x12, waiting for transfers between devices, to_plane(): lax.ppermute(value, 'col', [(index, index ^ partner) for index in range(4)])  3.44 us
  transfers between devices with their start and end apart: 26, of which 4 were waited for; matrix products, arithmetic and copies ran while one was open for 2% of the time, Pallas kernels for 53%

profile of v1, /device:TPU:0, one launch (start us, length us, event | category | flops | bytes accessed | tf_op | source)
XLA Modules:
  0.0 151.3 jit_solution(5510385566029952620)
XLA Ops:
  8.5 2.3 %fusion.4 = bf16[128,2048]{1,0:T(8,128)(2,1)} fusion(bf16[128,2048]{1,0:T(8,128)(2,1)} %refs_4_.6, bf16[128,2048]{1,0:T(8,128)(2,1)} %refs_3_.3), kind=kLoop, calls=%fused_computation.6 | loop fusion | flops 2097152 | bytes 1572864 | tf_op jit(solution)/shard_map/convert_element_type | solution.py:509
  10.9 4.7 %collective-permute-start.5 = (bf16[64,2048]{1,0:T(8,128)(2,1)S(1)}, bf16[64,2048]{1,0:T(8,128)(2,1)S(1)}, u32[]{:S(2)}, u32[]{:S(2)}) collective-permute-start(bf16[64,2048]{1,0:T(8,128)(2,1)S(1)} %collective-permute-done.refs_0_.refs_4_), channel_id=1, source_target_pairs={{0,24},{4,28},{8,16},{12,20},{16,8},{20,12},{24,0},{28,4},{1,25},{... | collective-permute-start | bytes 786440 | tf_op jit(solution)/shard_map/ppermute | solution.py:487
  16.2 14.9 %shard_map.102 = (bf16[2048,2048]{1,0:T(8,128)(2,1)}, bf16[2048,2048]{1,0:T(8,128)(2,1)}) custom-call(s32[3]{0:T(128)S(1)} %add_add_fusion.where, bf16[65536,128]{1,0:T(8,128)(2,1)} %bitcast.15), custom_call_target="tpu_custom_call" | custom-call | flops 34359738368 | bytes 268435456 | tf_op jit(solution)/shard_map/pallas_call | solution.py:20
  31.2 7.3 %collective-permute-done.3.refs_2_.refs_6_ = bf16[64,2048]{1,0:T(8,128)(2,1)S(1)} collective-permute-done((bf16[64,2048]{1,0:T(8,128)(2,1)S(1)}, bf16[64,2048]{1,0:T(8,128)(2,1)S(1)}, u32[]{:S(2)}, u32[]{:S(2)}) %collective-permute-start.3) | collective-permute-done | bytes 262176 | tf_op jit(solution)/shard_map/ppermute | solution.py:487
  38.6 6.4 %shard_map.103 = (f32[64,2048]{1,0:T(8,128)S(1)}, bf16[64,2048]{1,0:T(8,128)(2,1)}, bf16[64,2048]{1,0:T(8,128)(2,1)}, bf16[64,2048]{1,0:T(8,128)(2,1)}) custom-call(s32[3]{0:T(128)S(1)} %add_add_fusion.1.where, bf16[64,2048]{1,0:T(8,128)(2,1)S(1)} %collective-permute-done.refs_0_.refs_4_, bf16[64,2048]{1,0:T(8,128)(2,1)S(1)} %collective-permute-done.1.refs_1_.refs_5_, ...), custom_call_target="tpu_custom_call" | custom-call | flops 268435456 | bytes 1048576 | tf_op jit(solution)/shard_map/pallas_call | solution.py:20
  45.7 1.5 collective-permute-start.7
  47.2 1.5 %collective-permute-start.8 = (bf16[64,2048]{1,0:T(8,128)(2,1)}, bf16[64,2048]{1,0:T(8,128)(2,1)}, u32[]{:S(2)}, u32[]{:S(2)}) collective-permute-start(bf16[64,2048]{1,0:T(8,128)(2,1)} %get-tuple-element.60), channel_id=1, source_target_pairs={{0,2},{1,3},{2,0},{3,1},{4,6},{5,7},{6,4},{7,5},{8,10},{9,11},{10,... | collective-permute-start | bytes 786440 | tf_op jit(solution)/shard_map/ppermute | solution.py:483
  49.2 6.4 %shard_map.104 = (f32[64,2048]{1,0:T(8,128)S(1)}, bf16[64,2048]{1,0:T(8,128)(2,1)}, bf16[64,2048]{1,0:T(8,128)(2,1)}, bf16[64,2048]{1,0:T(8,128)(2,1)}) custom-call(s32[3]{0:T(128)S(1)} %add_add_fusion.where, bf16[64,2048]{1,0:T(8,128)(2,1)S(1)} %copy-done.3, bf16[64,2048]{1,0:T(8,128)(2,1)S(1)} %collective-permute-done.2.refs_1_, ...), custom_call_target="tpu_custom_call" | custom-call | flops 268435456 | bytes 1048576 | tf_op jit(solution)/shard_map/pallas_call | solution.py:20
  56.5 1.5 collective-permute-start.10
  58.0 1.5 %collective-permute-start.11 = (bf16[64,2048]{1,0:T(8,128)(2,1)}, bf16[64,2048]{1,0:T(8,128)(2,1)}, u32[]{:S(2)}, u32[]{:S(2)}) collective-permute-start(bf16[64,2048]{1,0:T(8,128)(2,1)} %get-tuple-element.67), channel_id=1, source_target_pairs={{0,2},{1,3},{2,0},{3,1},{4,6},{5,7},{6,4},{7,5},{8,10},{9,11},{10,... | collective-permute-start | bytes 786440 | tf_op jit(solution)/shard_map/ppermute | solution.py:483
  62.7 3.8 %shard_map.105 = (bf16[64,2048]{1,0:T(8,128)(2,1)S(1)}, bf16[128,2048]{1,0:T(8,128)(2,1)}) custom-call(s32[3]{0:T(128)S(1)} %add_add_fusion.1.where, f32[64,2048]{1,0:T(8,128)S(1)} %get-tuple-element.58.own, bf16[64,2048]{1,0:T(8,128)(2,1)S(1)} %copy-done.22, bf16[64,2048]{1,0:T(8,128)(2,1)} %collective-permute-done.8.refs_1_, ...), custom_call_target="tpu_custom_call" | custom-call | flops 16777216 | bytes 16777216 | tf_op jit(solution)/shard_map/pallas_call | solution.py:20
  66.5 1.4 collective-permute-start.18
  67.9 1.5 collective-permute-start.17
  70.0 1.6 %copy-done = bf16[512,2048]{1,0:T(8,128)(2,1)S(1)} copy-done((bf16[512,2048]{1,0:T(8,128)(2,1)S(1)}, bf16[512,2048]{1,0:T(8,128)(2,1)}, u32[]{:S(2)}) %copy-start) | copy-done | bytes 2097176
  71.7 8.6 %shard_map.106 = (f32[4,64,2048]{2,1,0:T(8,128)}, bf16[4,64,2048]{2,1,0:T(8,128)(2,1)}) custom-call(s32[3]{0:T(128)S(1)} %add_add_fusion.where, bf16[512,2048]{1,0:T(8,128)(2,1)S(1)} %copy-done, bf16[2048,2048]{1,0:T(8,128)(2,1)} %get-tuple-element.47.refs_1_), custom_call_target="tpu_custom_call" | custom-call | flops 536870912 | bytes 1048576 | tf_op jit(solution)/shard_map/pallas_call | solution.py:20
  80.3 3.9 %shard_map.107 = (bf16[64,2048]{1,0:T(8,128)(2,1)S(1)}, bf16[128,2048]{1,0:T(8,128)(2,1)}) custom-call(s32[3]{0:T(128)S(1)} %add_add_fusion.where, f32[64,2048]{1,0:T(8,128)S(1)} %copy-done.12, bf16[64,2048]{1,0:T(8,128)(2,1)} %collective-permute-done.10.refs_0_, bf16[64,2048]{1,0:T(8,128)(2,1)} %collective-permute-done.11.refs_1_, ...), custom_call_target="tpu_custom_call", output_to_operand_aliasing={{1}: (7, {})} | custom-call | flops 16777216 | bytes 16777216 | tf_op jit(solution)/shard_map/pallas_call | solution.py:20
  84.2 1.5 collective-permute-start.15
  87.8 6.9 %shard_map.109 = bf16[4,64,2048]{2,1,0:T(8,128)(2,1)S(1)} custom-call(s32[3]{0:T(128)S(1)} %add_add_fusion.1.where, bf16[64,2048]{1,0:T(8,128)(2,1)S(1)} %get-tuple-element.62.refs_0_.refs_5_, bf16[64,2048]{1,0:T(8,128)(2,1)S(1)} %collective-permute-done.16.refs_1_.refs_6_, bf16[64,2048]{1,0:T(8,128)(2,1)S(1)} %collective-permute-done.17.refs_2_.refs_7_, ...), custom_call_target="tpu_custom_call" | custom-call | flops 17179869184 | bytes 67108864 | tf_op jit(solution)/shard_map/pallas_call | solution.py:20
  94.9 2.4 %collective-permute-done.14.refs_2_.refs_3_ = bf16[64,2048]{1,0:T(8,128)(2,1)S(1)} collective-permute-done((bf16[64,2048]{1,0:T(8,128)(2,1)S(1)}, bf16[64,2048]{1,0:T(8,128)(2,1)S(1)}, u32[]{:S(2)}, u32[]{:S(2)}) %collective-permute-start.14) | collective-permute-done | bytes 262176 | tf_op jit(solution)/shard_map/ppermute | solution.py:483
  97.3 7.2 %shard_map.108.here = f32[4,64,2048]{2,1,0:T(8,128)S(1)} custom-call(s32[3]{0:T(128)S(1)} %add_add_fusion.where, bf16[64,2048]{1,0:T(8,128)(2,1)S(1)} %get-tuple-element.70.refs_0_.refs_1_, bf16[64,2048]{1,0:T(8,128)(2,1)S(1)} %collective-permute-done.13.refs_1_.refs_2_, bf16[64,2048]{1,0:T(8,128)(2,1)S(1)} %collective-permute-done.14.refs_2_.refs_3_, ...), custom_call_target="tpu_custom_call" | custom-call | flops 17179869184 | bytes 67108864 | tf_op jit(solution)/shard_map/pallas_call | solution.py:20
  104.5 2.2 %shard_map.110 = (f32[64,2048]{1,0:T(8,128)}, bf16[64,2048]{1,0:T(8,128)(2,1)S(1)}, bf16[64,2048]{1,0:T(8,128)(2,1)S(1)}, bf16[64,2048]{1,0:T(8,128)(2,1)S(1)}) custom-call(s32[3]{0:T(128)S(1)} %add_add_fusion.where, f32[4,64,2048]{2,1,0:T(8,128)S(1)} %shard_map.108.here, bf16[4,64,2048]{2,1,0:T(8,128)(2,1)S(1)} %collective-permute-done.19.there), custom_call_target="tpu_custom_call" | custom-call | flops 524288 | bytes 4718592 | tf_op jit(solution)/shard_map/pallas_call | solution.py:20
  106.7 3.1 %collective-permute-start.21 = (bf16[64,2048]{1,0:T(8,128)(2,1)S(1)}, bf16[64,2048]{1,0:T(8,128)(2,1)S(1)}, u32[]{:S(2)}, u32[]{:S(2)}) collective-permute-start(bf16[64,2048]{1,0:T(8,128)(2,1)S(1)} %get-tuple-element.79), channel_id=1, source_target_pairs={{0,16},{4,20},{8,24},{12,28},{16,0},{20,4},{24,8},{28,12},{1,17},{... | collective-permute-start | bytes 786440 | tf_op jit(solution)/shard_map/ppermute | solution.py:487
  111.1 20.0 %shard_map.111 = f32[65536,128]{1,0:T(8,128)} custom-call(s32[3]{0:T(128)S(1)} %add_add_fusion.where, bf16[512,2048]{1,0:T(8,128)(2,1)} %all-gather.4.cloned.1.call-done.refs_0_, bf16[64,2048]{1,0:T(8,128)(2,1)} %copy-done.17, bf16[64,2048]{1,0:T(8,128)(2,1)} %copy-done.20, bf16[64,2048]{1,0:T(8,128)(2,1)} %copy-done.19, bf16[64,2048]{1,0:T(8,128)(2,1)} %copy-done.18, ...), custom_call_target="tpu_custom_call" | custom-call | flops 8589934592 | bytes 39845888 | tf_op jit(solution)/shard_map/pallas_call | solution.py:20
  132.0 12.8 %shard_map.112 = f32[2048,2048]{1,0:T(8,128)} custom-call(s32[3]{0:T(128)S(1)} %add_add_fusion.where, bf16[64,2048]{1,0:T(8,128)(2,1)} %refs_0_.1, bf16[64,2048]{1,0:T(8,128)(2,1)} %copy-done.8, bf16[64,2048]{1,0:T(8,128)(2,1)} %copy-done.9, bf16[64,2048]{1,0:T(8,128)(2,1)} %copy-done.10, bf16[64,2048]{1,0:T(8,128)(2,1)} %copy-done.4, ...), custom_call_target="tpu_custom_call" | custom-call | flops 4294967296 | bytes 20971520 | tf_op jit(solution)/shard_map/pallas_call | solution.py:20
  (94 shorter events, 12.3 us)
Async XLA Ops:
  7.2 53.5 %all-gather.4.cloned.1.call-start = ((), (), s32[]{:S(2)}) async-start(), calls=%async_computation | async-start | bytes 2621440 | tf_op jit(solution)/shard_map/all_gather | solution.py:507
  7.9 79.2 %all-gather.6.cloned.1.call-start = ((), (), s32[]{:S(2)}) async-start(), calls=%async_computation.1 | async-start | bytes 2359296 | tf_op jit(solution)/shard_map/all_gather | solution.py:516
  10.9 20.3 %collective-permute-start.5 = (bf16[64,2048]{1,0:T(8,128)(2,1)S(1)}, bf16[64,2048]{1,0:T(8,128)(2,1)S(1)}, u32[]{:S(2)}, u32[]{:S(2)}) collective-permute-start(bf16[64,2048]{1,0:T(8,128)(2,1)S(1)} %collective-permute-done.refs_0_.refs_4_), channel_id=1, source_target_pairs={{0,24},{4,28},{8,16},{12,20},{16,8},{20,12},{24,0},{28,4},{1,25},{... | collective-permute-start | bytes 786440 | tf_op jit(solution)/shard_map/ppermute | solution.py:487
  15.6 23.0 %collective-permute-start.3 = (bf16[64,2048]{1,0:T(8,128)(2,1)S(1)}, bf16[64,2048]{1,0:T(8,128)(2,1)S(1)}, u32[]{:S(2)}, u32[]{:S(2)}) collective-permute-start(bf16[64,2048]{1,0:T(8,128)(2,1)S(1)} %collective-permute-done.refs_0_.refs_4_), channel_id=1, source_target_pairs={{0,16},{4,20},{8,24},{12,28},{16,0},{20,4},{24,8},{28,12},{1,17},{... | collective-permute-start | bytes 786440 | tf_op jit(solution)/shard_map/ppermute | solution.py:487
  15.6 23.0 %collective-permute-start.1 = (bf16[64,2048]{1,0:T(8,128)(2,1)S(1)}, bf16[64,2048]{1,0:T(8,128)(2,1)S(1)}, u32[]{:S(2)}, u32[]{:S(2)}) collective-permute-start(bf16[64,2048]{1,0:T(8,128)(2,1)S(1)} %collective-permute-done.refs_0_.refs_4_), channel_id=1, source_target_pairs={{0,8},{4,12},{8,0},{12,4},{16,24},{20,28},{24,16},{28,20},{1,9},{5... | collective-permute-start | bytes 786440 | tf_op jit(solution)/shard_map/ppermute | solution.py:487
  45.0 87.0 %all-gather.8.cloned.1.call-start = ((), (), s32[]{:S(2)}) async-start(), calls=%async_computation.2 | async-start | bytes 2621440 | tf_op jit(solution)/shard_map/all_gather | solution.py:532
  45.0 3.7 %collective-permute-start.2 = (bf16[64,2048]{1,0:T(8,128)(2,1)S(1)}, bf16[64,2048]{1,0:T(8,128)(2,1)S(1)}, u32[]{:S(2)}, u32[]{:S(2)}) collective-permute-start(bf16[64,2048]{1,0:T(8,128)(2,1)S(1)} %collective-permute-done.1.refs_1_.refs_5_), channel_id=1, source_target_pairs={{0,4},{4,0},{8,12},{12,8},{16,20},{20,16},{24,28},{28,24},{1,5},{5... | collective-permute-start | bytes 786440 | tf_op jit(solution)/shard_map/ppermute | solution.py:491
  45.1 4.1 %collective-permute-start.4 = (bf16[64,2048]{1,0:T(8,128)(2,1)S(1)}, bf16[64,2048]{1,0:T(8,128)(2,1)S(1)}, u32[]{:S(2)}, u32[]{:S(2)}) collective-permute-start(bf16[64,2048]{1,0:T(8,128)(2,1)S(1)} %collective-permute-done.3.refs_2_.refs_6_), channel_id=1, source_target_pairs={{0,4},{4,0},{8,12},{12,8},{16,20},{20,16},{24,28},{28,24},{1,5},{5... | collective-permute-start | bytes 786440 | tf_op jit(solution)/shard_map/ppermute | solution.py:491
  45.7 13.8 %collective-permute-start.7 = (bf16[64,2048]{1,0:T(8,128)(2,1)}, bf16[64,2048]{1,0:T(8,128)(2,1)S(1)}, u32[]{:S(2)}, u32[]{:S(2)}) collective-permute-start(bf16[64,2048]{1,0:T(8,128)(2,1)} %get-tuple-element.59), channel_id=1, source_target_pairs={{0,1},{1,0},{2,3},{3,2},{4,5},{5,4},{6,7},{7,6},{8,9},{9,8},{10,11... | collective-permute-start | bytes 786440 | tf_op jit(solution)/shard_map/ppermute | solution.py:483
  47.2 14.2 %collective-permute-start.8 = (bf16[64,2048]{1,0:T(8,128)(2,1)}, bf16[64,2048]{1,0:T(8,128)(2,1)}, u32[]{:S(2)}, u32[]{:S(2)}) collective-permute-start(bf16[64,2048]{1,0:T(8,128)(2,1)} %get-tuple-element.60), channel_id=1, source_target_pairs={{0,2},{1,3},{2,0},{3,1},{4,6},{5,7},{6,4},{7,5},{8,10},{9,11},{10,... | collective-permute-start | bytes 786440 | tf_op jit(solution)/shard_map/ppermute | solution.py:483
  48.7 13.0 %collective-permute-start.9 = (bf16[64,2048]{1,0:T(8,128)(2,1)}, bf16[64,2048]{1,0:T(8,128)(2,1)}, u32[]{:S(2)}, u32[]{:S(2)}) collective-permute-start(bf16[64,2048]{1,0:T(8,128)(2,1)} %get-tuple-element.61), channel_id=1, source_target_pairs={{0,3},{1,2},{2,1},{3,0},{4,7},{5,6},{6,5},{7,4},{8,11},{9,10},{10,... | collective-permute-start | bytes 786440 | tf_op jit(solution)/shard_map/ppermute | solution.py:483
  56.5 12.9 %collective-permute-start.10 = (bf16[64,2048]{1,0:T(8,128)(2,1)}, bf16[64,2048]{1,0:T(8,128)(2,1)}, u32[]{:S(2)}, u32[]{:S(2)}) collective-permute-start(bf16[64,2048]{1,0:T(8,128)(2,1)} %get-tuple-element.63), channel_id=1, source_target_pairs={{0,1},{1,0},{2,3},{3,2},{4,5},{5,4},{6,7},{7,6},{8,9},{9,8},{10,11... | collective-permute-start | bytes 786440 | tf_op jit(solution)/shard_map/ppermute | solution.py:483
  58.0 22.3 %collective-permute-start.11 = (bf16[64,2048]{1,0:T(8,128)(2,1)}, bf16[64,2048]{1,0:T(8,128)(2,1)}, u32[]{:S(2)}, u32[]{:S(2)}) collective-permute-start(bf16[64,2048]{1,0:T(8,128)(2,1)} %get-tuple-element.67), channel_id=1, source_target_pairs={{0,2},{1,3},{2,0},{3,1},{4,6},{5,7},{6,4},{7,5},{8,10},{9,11},{10,... | collective-permute-start | bytes 786440 | tf_op jit(solution)/shard_map/ppermute | solution.py:483
  60.2 20.1 %collective-permute-start.12 = (bf16[64,2048]{1,0:T(8,128)(2,1)}, bf16[64,2048]{1,0:T(8,128)(2,1)}, u32[]{:S(2)}, u32[]{:S(2)}) collective-permute-start(bf16[64,2048]{1,0:T(8,128)(2,1)} %get-tuple-element.68), channel_id=1, source_target_pairs={{0,3},{1,2},{2,1},{3,0},{4,7},{5,6},{6,5},{7,4},{8,11},{9,10},{10,... | collective-permute-start | bytes 786440 | tf_op jit(solution)/shard_map/ppermute | solution.py:483
  66.5 20.5 %collective-permute-start.18 = (bf16[64,2048]{1,0:T(8,128)(2,1)S(1)}, bf16[64,2048]{1,0:T(8,128)(2,1)S(1)}, u32[]{:S(2)}, u32[]{:S(2)}) collective-permute-start(bf16[64,2048]{1,0:T(8,128)(2,1)S(1)} %get-tuple-element.62.refs_0_.refs_5_), channel_id=1, source_target_pairs={{0,3},{1,2},{2,1},{3,0},{4,7},{5,6},{6,5},{7,4},{8,11},{9,10},{10,... | collective-permute-start | bytes 786440 | tf_op jit(solution)/shard_map/ppermute | solution.py:483
  67.9 19.8 %collective-permute-start.17 = (bf16[64,2048]{1,0:T(8,128)(2,1)S(1)}, bf16[64,2048]{1,0:T(8,128)(2,1)S(1)}, u32[]{:S(2)}, u32[]{:S(2)}) collective-permute-start(bf16[64,2048]{1,0:T(8,128)(2,1)S(1)} %get-tuple-element.62.refs_0_.refs_5_), channel_id=1, source_target_pairs={{0,2},{1,3},{2,0},{3,1},{4,6},{5,7},{6,4},{7,5},{8,10},{9,11},{10,... | collective-permute-start | bytes 786440 | tf_op jit(solution)/shard_map/ppermute | solution.py:483
  69.4 18.3 %collective-permute-start.16 = (bf16[64,2048]{1,0:T(8,128)(2,1)S(1)}, bf16[64,2048]{1,0:T(8,128)(2,1)S(1)}, u32[]{:S(2)}, u32[]{:S(2)}) collective-permute-start(bf16[64,2048]{1,0:T(8,128)(2,1)S(1)} %get-tuple-element.62.refs_0_.refs_5_), channel_id=1, source_target_pairs={{0,1},{1,0},{2,3},{3,2},{4,5},{5,4},{6,7},{7,6},{8,9},{9,8},{10,11... | collective-permute-start | bytes 786440 | tf_op jit(solution)/shard_map/ppermute | solution.py:483
  84.2 10.7 %collective-permute-start.15 = (bf16[64,2048]{1,0:T(8,128)(2,1)S(1)}, bf16[64,2048]{1,0:T(8,128)(2,1)S(1)}, u32[]{:S(2)}, u32[]{:S(2)}) collective-permute-start(bf16[64,2048]{1,0:T(8,128)(2,1)S(1)} %get-tuple-element.70.refs_0_.refs_1_), channel_id=1, source_target_pairs={{0,3},{1,2},{2,1},{3,0},{4,7},{5,6},{6,5},{7,4},{8,11},{9,10},{10,... | collective-permute-start | bytes 786440 | tf_op jit(solution)/shard_map/ppermute | solution.py:483
  85.6 11.6 %collective-permute-start.14 = (bf16[64,2048]{1,0:T(8,128)(2,1)S(1)}, bf16[64,2048]{1,0:T(8,128)(2,1)S(1)}, u32[]{:S(2)}, u32[]{:S(2)}) collective-permute-start(bf16[64,2048]{1,0:T(8,128)(2,1)S(1)} %get-tuple-element.70.refs_0_.refs_1_), channel_id=1, source_target_pairs={{0,2},{1,3},{2,0},{3,1},{4,6},{5,7},{6,4},{7,5},{8,10},{9,11},{10,... | collective-permute-start | bytes 786440 | tf_op jit(solution)/shard_map/ppermute | solution.py:483
  87.1 10.2 %collective-permute-start.13 = (bf16[64,2048]{1,0:T(8,128)(2,1)S(1)}, bf16[64,2048]{1,0:T(8,128)(2,1)S(1)}, u32[]{:S(2)}, u32[]{:S(2)}) collective-permute-start(bf16[64,2048]{1,0:T(8,128)(2,1)S(1)} %get-tuple-element.70.refs_0_.refs_1_), channel_id=1, source_target_pairs={{0,1},{1,0},{2,3},{3,2},{4,5},{5,4},{6,7},{7,6},{8,9},{9,8},{10,11... | collective-permute-start | bytes 786440 | tf_op jit(solution)/shard_map/ppermute | solution.py:483
  94.8 9.7 %collective-permute-start.19 = (bf16[4,64,2048]{2,1,0:T(8,128)(2,1)S(1)}, bf16[4,64,2048]{2,1,0:T(8,128)(2,1)S(1)}, u32[]{:S(2)}, u32[]{:S(2)}) collective-permute-start(bf16[4,64,2048]{2,1,0:T(8,128)(2,1)S(1)} %shard_map.109), channel_id=1, source_target_pairs={{0,4},{4,0},{8,12},{12,8},{16,20},{20,16},{24,28},{28,24},{1,5},{5... | collective-permute-start | bytes 3145736 | tf_op jit(solution)/shard_map/ppermute | solution.py:491
  106.7 24.4 %collective-permute-start.20 = (bf16[64,2048]{1,0:T(8,128)(2,1)S(1)}, bf16[64,2048]{1,0:T(8,128)(2,1)S(1)}, u32[]{:S(2)}, u32[]{:S(2)}) collective-permute-start(bf16[64,2048]{1,0:T(8,128)(2,1)S(1)} %get-tuple-element.78), channel_id=1, source_target_pairs={{0,8},{4,12},{8,0},{12,4},{16,24},{20,28},{24,16},{28,20},{1,9},{5... | collective-permute-start | bytes 786440 | tf_op jit(solution)/shard_map/ppermute | solution.py:487
  106.7 24.4 %collective-permute-start.21 = (bf16[64,2048]{1,0:T(8,128)(2,1)S(1)}, bf16[64,2048]{1,0:T(8,128)(2,1)S(1)}, u32[]{:S(2)}, u32[]{:S(2)}) collective-permute-start(bf16[64,2048]{1,0:T(8,128)(2,1)S(1)} %get-tuple-element.79), channel_id=1, source_target_pairs={{0,16},{4,20},{8,24},{12,28},{16,0},{20,4},{24,8},{28,12},{1,17},{... | collective-permute-start | bytes 786440 | tf_op jit(solution)/shard_map/ppermute | solution.py:487
  109.8 21.3 %collective-permute-start.22 = (bf16[64,2048]{1,0:T(8,128)(2,1)S(1)}, bf16[64,2048]{1,0:T(8,128)(2,1)S(1)}, u32[]{:S(2)}, u32[]{:S(2)}) collective-permute-start(bf16[64,2048]{1,0:T(8,128)(2,1)S(1)} %get-tuple-element.80), channel_id=1, source_target_pairs={{0,24},{4,28},{8,16},{12,20},{16,8},{20,12},{24,0},{28,4},{1,25},{... | collective-permute-start | bytes 786440 | tf_op jit(solution)/shard_map/ppermute | solution.py:487
  (26 other events, 402.1 us)
Sparse Core Ops, SparseCore 0:
  9.8 38.0 all-gather.3
  49.5 29.7 all-gather.5
  94.9 34.9 all-gather.7

commit v2 on v1

--- a/solution.py
+++ b/solution.py
@@ -37,23 +37,14 @@
     return [pl.BlockSpec(memory_space=pl.ANY) for _ in pieces]
 
 
-def lay(moves, sems, groups=1):
-    first = pl.program_id(0) == 0
-    copies = [pltpu.make_async_copy(piece, place, sems.at[index]) for index, (piece, place) in enumerate(moves)]
-    size = len(copies) // groups
-
-    @pl.when(first)
-    def _():
+def lay(moves, sems):
+    @pl.when(pl.program_id(0) == 0)
+    def _():
+        copies = [pltpu.make_async_copy(piece, place, sems.at[index]) for index, (piece, place) in enumerate(moves)]
         for copy in copies:
             copy.start()
-
-    def arrived(group):
-        @pl.when(first)
-        def _():
-            for copy in copies[group * size : (group + 1) * size]:
-                copy.wait()
-
-    return arrived
+        for copy in copies:
+            copy.wait()
 
 
 DEPTH = 3
@@ -159,11 +150,18 @@
 
 
 def share_body(where, *refs):
-    pieces, source, own, sends, rows, sems, buffers = refs[:4], refs[4], refs[5], refs[6:9], *refs[9:11], refs[11:]
+    pieces, rest, source, own, sends, rows, sems, buffers = refs[:4], *refs[4:7], refs[7:10], *refs[10:12], refs[12:]
     block = buffers[0].shape[1]
     weight = stream(lambda step: source.at[at(step * block, block)], *buffers)
     first = where[COLUMN] ^ where[CHIP]
-    lay([(piece, rows.at[at((first ^ index) * 64, 64)]) for index, piece in enumerate(pieces)], sems)(0)
+    near = pieces[0].shape[1]
+    far_columns = pl.ds(near, rest.shape[1])
+    moves = []
+    for index, piece in enumerate(pieces):
+        moves.append((piece, rows.at[at((first ^ index) * 64, 64), pl.ds(0, near)]))
+        here = at((where[COLUMN] ^ index) * 128 + where[CORE] * 64, 64)
+        moves.append((rest.at[here], rows.at[pl.ds(index * 64, 64), far_columns]))
+    lay(moves, sems)
 
     total = dot_turned(rows[...], weight[...])
     own[...] = total[:64]
@@ -171,22 +169,21 @@
         send[...] = total[(index + 1) * 64 : (index + 2) * 64].astype(BF16)
 
 
-def share(where, pieces, weight):
+def share(where, pieces, rest, weight, own, send):
     channels, features = weight.shape
     block = 512
     spec = pl.BlockSpec((64, block), lambda i, *_: (0, i))
-    own, send = jax.ShapeDtypeStruct((64, channels), F32), pltpu.HBM((64, channels), BF16)
     return run(
         share_body,
         where,
-        (*pieces, stay(weight)),
-        far(pieces) + [HBM],
-        [own, send, send, send],
+        (*pieces, stay(rest), stay(weight)),
+        far(pieces) + [HBM, HBM],
+        [own((64, channels), F32)] + [send((64, channels), BF16)] * 3,
         [spec] * 4,
         (channels // block,),
         scratch=[
             pltpu.VMEM((256, features), BF16),
-            pltpu.SemaphoreType.DMA((4,)),
+            pltpu.SemaphoreType.DMA((8,)),
             *streamed((block, features), BF16),
         ],
         flops=2 * 256 * channels * features // WEIGHT,
@@ -209,7 +206,7 @@
 
 def gate_step(where, own, received, scan, gate, previous):
     channels = scan.shape[1]
-    block = 512
+    block = channels
     spec = pl.BlockSpec((64, block), lambda i, *_: (0, i))
     mine = pl.BlockSpec((64, block), lambda i, where: (where[CORE], i))
     args = [own, *received, scan, gate]
@@ -243,7 +240,7 @@
         start = (where[CHIP] ^ index) * 128
         moves.append((branch.at[at(start + core * 64, 64)], rows.at[pl.ds(index * 64, 64)]))
         moves.append((branch.at[at(start + (1 - core) * 64, 64)], rows.at[pl.ds(256 + index * 64, 64)]))
-    lay(moves, sems)(0)
+    lay(moves, sems)
     total = dot_nt(rows[...], weight[...])
     mine[...] = total[:256].reshape(mine.shape)
     other[...] = total[256:].reshape(other.shape).astype(BF16)
@@ -276,7 +273,7 @@
     block = buffers[0].shape[1]
     weight = stream(lambda step: source.at[at(step * block, block)], *buffers)
     first = where[COLUMN] ^ where[CHIP]
-    lay([(piece, rows.at[at((first ^ index) * 64, 64)]) for index, piece in enumerate(pieces)], sems)(0)
+    lay([(piece, rows.at[at((first ^ index) * 64, 64)]) for index, piece in enumerate(pieces)], sems)
     total = dot_turned(rows[...], weight[...])
     out[...] = (total.reshape(out.shape) + branch[...].astype(F32)).astype(out.dtype)
 
@@ -310,7 +307,7 @@
 
 def combine(where, here, there):
     features = here.shape[2]
-    block = 512
+    block = features
     four = pl.BlockSpec((4, 64, block), lambda i, *_: (0, 0, i))
     one = pl.BlockSpec((64, block), lambda i, *_: (0, i))
     return run(
@@ -332,12 +329,12 @@
     slot = lax.rem(step, 2)
     group, lines = block // 8, 2 * tiles
     pitch = group * lines + 1
-    moves = [(branch.at[pl.ds(start, 64)], rows.at[0, pl.ds(start, 64)]) for start in range(0, 512, 64)]
+    moves = [(branch.at[pl.ds(start, 128)], rows.at[0, pl.ds(start, 128)]) for start in range(0, 512, 128)]
     for index in range(4):
         start = (where[COLUMN] ^ index) * 128
         moves.append((mine[index], rows.at[1, at(start + where[CORE] * 64, 64)]))
         moves.append((other[index], rows.at[1, at(start + (1 - where[CORE]) * 64, 64)]))
-    arrived = lay(moves, sems, 2)
+    lay(moves, sems)
 
     @pl.when(step == 0)
     def _():
@@ -360,7 +357,6 @@
     left = dot_nt(order[...], saved[...]).astype(BF16)
     width = 256
     for half in range(2):
-        arrived(half)
         for first in range(0, tiles * LANES, width):
             total = dot_nn(left, rows[half, :, first : first + width])
             for tile in range(width // LANES):
@@ -399,7 +395,7 @@
             pltpu.VMEM((2, tokens, channels), BF16),
             pltpu.VMEM((block, block), BF16),
             pltpu.VMEM((2, held, LANES), F32),
-            pltpu.SemaphoreType.DMA((16,)),
+            pltpu.SemaphoreType.DMA((12,)),
             pltpu.SemaphoreType.DMA((2, 8)),
         ],
         flops=4 * tokens * features * channels,
@@ -410,68 +406,46 @@
 
 
 def out_grad_body(where, *refs):
-    mine, other, gated, out, right, same, held, sems, out_sems = refs[:4], refs[4:8], *refs[8:]
-    step, steps = pl.program_id(0), pl.num_programs(0)
-    slot = lax.rem(step, 2)
-    _, columns, block, width = held.shape
-    moves = []
+    mine, other, rest, gated, out, right, same, sems = refs[:4], refs[4:8], *refs[8:]
+    block = same.shape[0]
+    near = pl.ds(0, mine[0].shape[1])
+    moves = [(rest, right.at[:, pl.ds(mine[0].shape[1], rest.shape[1])])]
     for index in range(4):
         start = (where[CHIP] ^ index) * 128
-        moves.append((mine[index], right.at[at(start + where[CORE] * 64, 64)]))
-        moves.append((other[index], right.at[at(start + (1 - where[CORE]) * 64, 64)]))
-    arrived = lay(moves, sems)
-
-    @pl.when(step == 0)
+        moves.append((mine[index], right.at[at(start + where[CORE] * 64, 64), near]))
+        moves.append((other[index], right.at[at(start + (1 - where[CORE]) * 64, 64), near]))
+    lay(moves, sems)
+
+    @pl.when(pl.program_id(0) == 0)
     def _():
         row = lax.broadcasted_iota(jnp.int32, (block, block), 0)
         column = lax.broadcasted_iota(jnp.int32, (block, block), 1)
         same[...] = jnp.where(row == column, 1.0, 0.0).astype(BF16)
 
-    def copy(step, slot, part):
-        return pltpu.make_async_copy(
-            held.at[slot, part],
-            out.at[at(step * block, block), pl.ds(part * width, width)],
-            out_sems.at[slot, part],
-        )
-
     rows = dot_nt(same[...], gated[...]).astype(BF16)
-    arrived(0)
-    for part in range(columns):
-
-        @pl.when(step >= 2)
-        def _():
-            copy(step - 2, slot, part).wait()
-
-        held[slot, part] = dot_nn(rows, right[:, part * width : (part + 1) * width])
-        copy(step, slot, part).start()
-
-    @pl.when(step == steps - 1)
-    def _():
-        for part in range(columns):
-            copy(step - 1, 1 - slot, part).wait()
-        for part in range(columns):
-            copy(step, slot, part).wait()
-
-
-def out_grad(where, gated, mine, other):
+    width = 512
+    for first in range(0, out.shape[1], width):
+        here = slice(first, first + width)
+        out[:, here] = dot_nn(rows, right[:, here])
+
+
+def out_grad(where, gated, mine, other, rest):
     tokens, channels = gated.shape
-    features = mine[0].shape[1]
-    block, width = 512, 512
+    features = mine[0].shape[1] + rest.shape[1]
+    block = 512
     pieces = (*mine, *other)
     return run(
         out_grad_body,
         where,
-        tuple(map(stay, (*pieces, gated))),
-        far(pieces) + [pl.BlockSpec((tokens, block), lambda i, *_: (0, i))],
+        tuple(map(stay, (*pieces, rest, gated))),
+        far(pieces) + [HBM, pl.BlockSpec((tokens, block), lambda i, *_: (0, i))],
         jax.ShapeDtypeStruct((channels, features), F32),
-        pl.BlockSpec(memory_space=pl.ANY),
+        pl.BlockSpec((block, features), lambda i, *_: (i, 0)),
         (channels // block,),
         scratch=[
             pltpu.VMEM((tokens, features), BF16),
             pltpu.VMEM((block, block), BF16),
-            pltpu.VMEM((2, features // width, block, width), F32),
-            pltpu.SemaphoreType.DMA((8,)),
-            pltpu.SemaphoreType.DMA((2, features // width)),
+            pltpu.SemaphoreType.DMA((9,)),
         ],
         flops=2 * tokens * channels * features,
         moved=4 * channels * features + 2 * tokens * (channels + features),
@@ -503,16 +477,19 @@
     mine = jnp.stack([column, core, chip]).astype(jnp.int32)
     other = jnp.stack([column, 1 - core, chip]).astype(jnp.int32)
 
-    beside = to_other_core(out_cotangent)
-    branch = lax.all_gather(branch_grad, "col", axis=0, tiled=True)
+    near = out_cotangent.shape[1] * 3 // 4
+    rest = lax.all_gather(out_cotangent[:, near:], "row", axis=0, tiled=True)
+    own_near = out_cotangent[:, :near]
+    beside = to_other_core(own_near)
+    branch = lax.all_gather(after(branch_grad, beside), "col", axis=0, tiled=True)
     gate_value = gate_input.astype(F32)
     gated = (scan_output.astype(F32) * (gate_value * jax.nn.sigmoid(gate_value))).astype(BF16)
     branch_weight, gate_weight = split_weight(mine, after(in_weight, beside, gated))
     cot_other = (beside, *(to_chip(beside, partner) for partner in PARTNERS))
-    cot_mine = (out_cotangent, *(to_other_core(after(block, branch_weight)) for block in cot_other[1:]))
-
-    share_other = share(other, cot_other, after(out_weight, branch_weight))
-    share_mine = share(mine, after(cot_mine, share_other[0]), out_weight)
+    cot_mine = (own_near, *(to_other_core(after(block, branch_weight)) for block in cot_other[1:]))
+
+    share_other = share(other, cot_other, rest, after(out_weight, branch_weight), jax.ShapeDtypeStruct, pltpu.HBM)
+    share_mine = share(mine, after(cot_mine, share_other[0]), rest, out_weight, pltpu.HBM, jax.ShapeDtypeStruct)
     saved = lax.all_gather(after(saved_input, share_other[0]), "row", axis=0, tiled=True)
     sums_other = [to_plane(send, partner) for send, partner in zip(share_other[1:], PARTNERS)]
     sums_mine = [to_plane(send, partner) for send, partner in zip(share_mine[1:], PARTNERS)]
@@ -532,7 +509,7 @@
     gated = lax.all_gather(after(gated, there), "col", axis=0, tiled=True)
     in_weight_grad = in_grad(mine, branch, grad_mine, grad_other, after(saved, total))
     in_weight_grad, total = lax.optimization_barrier((in_weight_grad, total))
-    out_weight_grad = out_grad(mine, gated, after(cot_mine, total), cot_other)
+    out_weight_grad = out_grad(mine, gated, after(cot_mine, total), cot_other, rest)
     for term in terms:
         total = total + term.astype(F32)
     return (total.astype(BF16), scan_grad, in_weight_grad, out_weight_grad)

time: 152 us -> 165 us (1.086)
  blocking collectives: 0 us -> 17.2 us
  waiting for transfers between devices: 11.5 us -> 7.4 us
  Pallas kernels: 93.1 us -> 91.1 us
  local copies, waits for them, and re-layouts: 4.17 us -> 6.13 us
    all_gather x0 -> x1, blocking collectives: none -> 17.2 us  [plane_per_device(): rest = lax.all_gather(out_cotangent[:, near:], 'row', axis=0, tiled=True)]
    ppermute x6, waiting for transfers between devices: 7.35 us -> 2.23 us  [to_chip(): lax.ppermute(value, 'row', [(index, index ^ 2 * partner) for index in ran...]
    pallas_call x11, Pallas kernels: 93.1 us -> 91.1 us  [run(): pl.pallas_call(body, out_shape=outs, grid_spec=pltpu.PrefetchScalarGridSp...]
    slice x0 -> x2, local copies, waits for them, and re-layouts: none -> 1.79 us  [the longest x1 0.94 us: plane_per_device(): own_near = out_cotangent[:, :near]]
  transfers between devices with their start and end apart: 26 -> 26, of which waited for: 4 -> 4; matrix products, arithmetic and copies ran while one was open for 2% -> 3% of each run, Pallas kernels for 53% -> 48%
where the time goes in v2:
time: 165 us; the launch traced here: 164 us
  Pallas kernels  91.1 us (55%)
  starting transfers between devices  24.4 us (15%)
  blocking collectives  17.2 us (10%)
  between operations  14.2 us (9%)
  waiting for transfers between devices  7.4 us (4%)
  local copies, waits for them, and re-layouts  6.13 us (4%)
  other arithmetic  3.29 us (2%)
    pallas_call x11, Pallas kernels, run(): pl.pallas_call(body, out_shape=outs, grid_spec=pltpu.PrefetchScalarGridSp...  91.1 us
    all_gather x1, blocking collectives, plane_per_device(): rest = lax.all_gather(out_cotangent[:, near:], 'row', axis=0, tiled=True)  17.2 us
    ppermute x12, starting transfers between devices, to_plane(): lax.ppermute(value, 'col', [(index, index ^ partner) for index in range(4)])  14 us
    ppermute x6, starting transfers between devices, to_chip(): lax.ppermute(value, 'row', [(index, index ^ 2 * partner) for index in ran...  8.84 us
    unnamed x48, local copies, waits for them, and re-layouts  4.34 us
    ppermute x12, waiting for transfers between devices, to_plane(): lax.ppermute(value, 'col', [(index, index ^ partner) for index in range(4)])  4.01 us
  transfers between devices with their start and end apart: 26, of which 4 were waited for; matrix products, arithmetic and copies ran while one was open for 3% of the time, Pallas kernels for 48%

profile of v2, /device:TPU:0, one launch (start us, length us, event | category | flops | bytes accessed | tf_op | source)
XLA Modules:
  0.0 163.6 jit_solution(6630401058089929129)
XLA Ops:
  9.7 2.3 %fusion.4 = bf16[128,2048]{1,0:T(8,128)(2,1)} fusion(bf16[128,2048]{1,0:T(8,128)(2,1)} %refs_4_.3, bf16[128,2048]{1,0:T(8,128)(2,1)} %refs_3_.3), kind=kLoop, calls=%fused_computation.6 | loop fusion | flops 2097152 | bytes 1572864 | tf_op jit(solution)/shard_map/convert_element_type | solution.py:486
  12.0 17.2 %all_gather.13.refs_4_.refs_8_ = bf16[512,512]{1,0:T(8,128)(2,1)} all-gather(bf16[64,512]{1,0:T(8,128)(2,1)S(1)} %slice.7), channel_id=1, replica_groups=mesh['row'=8,'col'=4] {'row'}, dimensions={0}, use_global_device_ids=true | all-gather | bytes 589824 | tf_op jit(solution)/shard_map/all_gather | solution.py:481
  29.3 3.6 %collective-permute-start.5 = (bf16[64,1536]{1,0:T(8,128)(2,1)S(1)}, bf16[64,1536]{1,0:T(8,128)(2,1)S(1)}, u32[]{:S(2)}, u32[]{:S(2)}) collective-permute-start(bf16[64,1536]{1,0:T(8,128)(2,1)S(1)} %collective-permute-done.refs_0_.refs_4_), channel_id=1, source_target_pairs={{0,24},{4,28},{8,16},{12,20},{16,8},{20,12},{24,0},{28,4},{1,25},{... | collective-permute-start | bytes 589832 | tf_op jit(solution)/shard_map/ppermute | solution.py:461
  33.7 14.2 %shard_map.102 = (bf16[2048,2048]{1,0:T(8,128)(2,1)}, bf16[2048,2048]{1,0:T(8,128)(2,1)}) custom-call(s32[3]{0:T(128)S(1)} %add_add_fusion.where, bf16[65536,128]{1,0:T(8,128)(2,1)} %bitcast.15), custom_call_target="tpu_custom_call" | custom-call | flops 34359738368 | bytes 268435456 | tf_op jit(solution)/shard_map/pallas_call | solution.py:20
  48.0 2.2 %collective-permute-done.3.refs_2_.refs_6_ = bf16[64,1536]{1,0:T(8,128)(2,1)S(1)} collective-permute-done((bf16[64,1536]{1,0:T(8,128)(2,1)S(1)}, bf16[64,1536]{1,0:T(8,128)(2,1)S(1)}, u32[]{:S(2)}, u32[]{:S(2)}) %collective-permute-start.3) | collective-permute-done | bytes 196640 | tf_op jit(solution)/shard_map/ppermute | solution.py:461
  50.2 8.1 %shard_map.103 = (f32[64,2048]{1,0:T(8,128)S(1)}, bf16[64,2048]{1,0:T(8,128)(2,1)}, bf16[64,2048]{1,0:T(8,128)(2,1)}, bf16[64,2048]{1,0:T(8,128)(2,1)}) custom-call(s32[3]{0:T(128)S(1)} %add_add_fusion.1.where, bf16[64,1536]{1,0:T(8,128)(2,1)S(1)} %collective-permute-done.refs_0_.refs_4_, bf16[64,1536]{1,0:T(8,128)(2,1)S(1)} %collective-permute-done.1.refs_1_.refs_5_, ...), custom_call_target="tpu_custom_call" | custom-call | flops 268435456 | bytes 1048576 | tf_op jit(solution)/shard_map/pallas_call | solution.py:20
  59.3 1.5 collective-permute-start.7
  60.7 1.5 collective-permute-start.8
  62.8 7.9 %shard_map.104 = (f32[64,2048]{1,0:T(8,128)}, bf16[64,2048]{1,0:T(8,128)(2,1)}, bf16[64,2048]{1,0:T(8,128)(2,1)}, bf16[64,2048]{1,0:T(8,128)(2,1)}) custom-call(s32[3]{0:T(128)S(1)} %add_add_fusion.where, bf16[64,1536]{1,0:T(8,128)(2,1)S(1)} %slice.6.refs_0_, bf16[64,1536]{1,0:T(8,128)(2,1)S(1)} %collective-permute-done.2.refs_1_, ...), custom_call_target="tpu_custom_call" | custom-call | flops 268435456 | bytes 1048576 | tf_op jit(solution)/shard_map/pallas_call | solution.py:20
  70.7 1.5 collective-permute-start.10
  72.2 1.5 collective-permute-start.11
  75.0 3.0 %collective-permute-done.9.refs_2_ = bf16[64,2048]{1,0:T(8,128)(2,1)} collective-permute-done((bf16[64,2048]{1,0:T(8,128)(2,1)}, bf16[64,2048]{1,0:T(8,128)(2,1)}, u32[]{:S(2)}, u32[]{:S(2)}) %collective-permute-start.9) | collective-permute-done | bytes 262176 | tf_op jit(solution)/shard_map/ppermute | solution.py:457
  79.0 2.5 %shard_map.105 = (bf16[64,2048]{1,0:T(8,128)(2,1)S(1)}, bf16[128,2048]{1,0:T(8,128)(2,1)}) custom-call(s32[3]{0:T(128)S(1)} %add_add_fusion.1.where, f32[64,2048]{1,0:T(8,128)S(1)} %get-tuple-element.60.own, bf16[64,2048]{1,0:T(8,128)(2,1)S(1)} %copy-done.21, bf16[64,2048]{1,0:T(8,128)(2,1)} %collective-permute-done.8.refs_1_, ...), custom_call_target="tpu_custom_call" | custom-call | flops 16777216 | bytes 16777216 | tf_op jit(solution)/shard_map/pallas_call | solution.py:20
  81.8 1.6 %collective-permute-start.17 = (bf16[64,2048]{1,0:T(8,128)(2,1)S(1)}, bf16[64,2048]{1,0:T(8,128)(2,1)S(1)}, u32[]{:S(2)}, u32[]{:S(2)}) collective-permute-start(bf16[64,2048]{1,0:T(8,128)(2,1)S(1)} %get-tuple-element.64.refs_0_.refs_5_), channel_id=1, source_target_pairs={{0,2},{1,3},{2,0},{3,1},{4,6},{5,7},{6,4},{7,5},{8,10},{9,11},{10,... | collective-permute-start | bytes 786440 | tf_op jit(solution)/shard_map/ppermute | solution.py:457
  83.5 1.5 collective-permute-start.16
  85.0 1.6 copy-done
  86.6 8.6 %shard_map.106 = (f32[4,64,2048]{2,1,0:T(8,128)}, bf16[4,64,2048]{2,1,0:T(8,128)(2,1)}) custom-call(s32[3]{0:T(128)S(1)} %add_add_fusion.where, bf16[512,2048]{1,0:T(8,128)(2,1)S(1)} %copy-done, bf16[2048,2048]{1,0:T(8,128)(2,1)} %get-tuple-element.49.refs_1_), custom_call_target="tpu_custom_call" | custom-call | flops 536870912 | bytes 1048576 | tf_op jit(solution)/shard_map/pallas_call | solution.py:20
  95.2 2.6 %shard_map.107 = (bf16[64,2048]{1,0:T(8,128)(2,1)S(1)}, bf16[128,2048]{1,0:T(8,128)(2,1)}) custom-call(s32[3]{0:T(128)S(1)} %add_add_fusion.where, f32[64,2048]{1,0:T(8,128)S(1)} %copy-done.11, bf16[64,2048]{1,0:T(8,128)(2,1)} %collective-permute-done.10.refs_0_, bf16[64,2048]{1,0:T(8,128)(2,1)} %collective-permute-done.11.refs_1_, ...), custom_call_target="tpu_custom_call", output_to_operand_aliasing={{1}: (7, {})} | custom-call | flops 16777216 | bytes 16777216 | tf_op jit(solution)/shard_map/pallas_call | solution.py:20
  102.4 6.9 %shard_map.109 = bf16[4,64,2048]{2,1,0:T(8,128)(2,1)S(1)} custom-call(s32[3]{0:T(128)S(1)} %add_add_fusion.1.where, bf16[64,2048]{1,0:T(8,128)(2,1)S(1)} %get-tuple-element.64.refs_0_.refs_5_, bf16[64,2048]{1,0:T(8,128)(2,1)S(1)} %collective-permute-done.16.refs_1_.refs_6_, bf16[64,2048]{1,0:T(8,128)(2,1)S(1)} %collective-permute-done.17.refs_2_.refs_7_, ...), custom_call_target="tpu_custom_call" | custom-call | flops 17179869184 | bytes 67108864 | tf_op jit(solution)/shard_map/pallas_call | solution.py:20
  111.5 7.3 %shard_map.108.here = f32[4,64,2048]{2,1,0:T(8,128)S(1)} custom-call(s32[3]{0:T(128)S(1)} %add_add_fusion.where, bf16[64,2048]{1,0:T(8,128)(2,1)S(1)} %get-tuple-element.72.refs_0_.refs_1_, bf16[64,2048]{1,0:T(8,128)(2,1)S(1)} %collective-permute-done.13.refs_1_.refs_2_, bf16[64,2048]{1,0:T(8,128)(2,1)S(1)} %collective-permute-done.14.refs_2_.refs_3_, ...), custom_call_target="tpu_custom_call" | custom-call | flops 17179869184 | bytes 67108864 | tf_op jit(solution)/shard_map/pallas_call | solution.py:20
  120.3 1.5 collective-permute-start.20
  121.8 2.4 %collective-permute-start.21 = (bf16[64,2048]{1,0:T(8,128)(2,1)S(1)}, bf16[64,2048]{1,0:T(8,128)(2,1)S(1)}, u32[]{:S(2)}, u32[]{:S(2)}) collective-permute-start(bf16[64,2048]{1,0:T(8,128)(2,1)S(1)} %get-tuple-element.81), channel_id=1, source_target_pairs={{0,16},{4,20},{8,24},{12,28},{16,0},{20,4},{24,8},{28,12},{1,17},{... | collective-permute-start | bytes 786440 | tf_op jit(solution)/shard_map/ppermute | solution.py:461
  124.7 19.5 %shard_map.111 = f32[65536,128]{1,0:T(8,128)} custom-call(s32[3]{0:T(128)S(1)} %add_add_fusion.where, bf16[512,2048]{1,0:T(8,128)(2,1)} %all-gather.4.cloned.1.call-done.refs_0_, bf16[64,2048]{1,0:T(8,128)(2,1)} %copy-done.16, bf16[64,2048]{1,0:T(8,128)(2,1)} %copy-done.19, bf16[64,2048]{1,0:T(8,128)(2,1)} %copy-done.18, bf16[64,2048]{1,0:T(8,128)(2,1)} %copy-done.17, ...), custom_call_target="tpu_custom_call" | custom-call | flops 8589934592 | bytes 39845888 | tf_op jit(solution)/shard_map/pallas_call | solution.py:20
  145.1 12.0 %shard_map.112 = f32[2048,2048]{1,0:T(8,128)} custom-call(s32[3]{0:T(128)S(1)} %add_add_fusion.where, bf16[64,1536]{1,0:T(8,128)(2,1)} %copy-done.3, bf16[64,1536]{1,0:T(8,128)(2,1)} %copy-done.8, bf16[64,1536]{1,0:T(8,128)(2,1)} %copy-done.9, bf16[64,1536]{1,0:T(8,128)(2,1)} %copy-done.10, bf16[64,1536]{1,0:T(8,128)(2,1)} %copy-done.4, ...), custom_call_target="tpu_custom_call" | custom-call | flops 4294967296 | bytes 20971520 | tf_op jit(solution)/shard_map/pallas_call | solution.py:20
  (97 shorter events, 16.8 us)
Async XLA Ops:
  7.2 67.8 %all-gather.4.cloned.1.call-start = ((), (), s32[]{:S(2)}) async-start(), calls=%async_computation | async-start | bytes 2621440 | tf_op jit(solution)/shard_map/all_gather | solution.py:484
  8.2 21.0 %collective-permute-start = (bf16[64,1536]{1,0:T(8,128)(2,1)S(1)}, bf16[64,1536]{1,0:T(8,128)(2,1)S(1)}, u32[]{:S(2)}, u32[]{:S(2)}) collective-permute-start(bf16[64,1536]{1,0:T(8,128)(2,1)S(1)} %slice.6.refs_0_), channel_id=1, source_target_pairs={{0,4},{4,0},{8,12},{12,8},{16,20},{20,16},{24,28},{28,24},{1,5},{5... | collective-permute-start | bytes 589832 | tf_op jit(solution)/shard_map/ppermute | solution.py:465
  29.2 71.7 %all-gather.6.cloned.1.call-start = ((), (), s32[]{:S(2)}) async-start(), calls=%async_computation.1 | async-start | bytes 2359296 | tf_op jit(solution)/shard_map/all_gather | solution.py:493
  29.3 18.7 %collective-permute-start.5 = (bf16[64,1536]{1,0:T(8,128)(2,1)S(1)}, bf16[64,1536]{1,0:T(8,128)(2,1)S(1)}, u32[]{:S(2)}, u32[]{:S(2)}) collective-permute-start(bf16[64,1536]{1,0:T(8,128)(2,1)S(1)} %collective-permute-done.refs_0_.refs_4_), channel_id=1, source_target_pairs={{0,24},{4,28},{8,16},{12,20},{16,8},{20,12},{24,0},{28,4},{1,25},{... | collective-permute-start | bytes 589832 | tf_op jit(solution)/shard_map/ppermute | solution.py:461
  32.8 17.3 %collective-permute-start.3 = (bf16[64,1536]{1,0:T(8,128)(2,1)S(1)}, bf16[64,1536]{1,0:T(8,128)(2,1)S(1)}, u32[]{:S(2)}, u32[]{:S(2)}) collective-permute-start(bf16[64,1536]{1,0:T(8,128)(2,1)S(1)} %collective-permute-done.refs_0_.refs_4_), channel_id=1, source_target_pairs={{0,16},{4,20},{8,24},{12,28},{16,0},{20,4},{24,8},{28,12},{1,17},{... | collective-permute-start | bytes 589832 | tf_op jit(solution)/shard_map/ppermute | solution.py:461
  32.8 17.3 %collective-permute-start.1 = (bf16[64,1536]{1,0:T(8,128)(2,1)S(1)}, bf16[64,1536]{1,0:T(8,128)(2,1)S(1)}, u32[]{:S(2)}, u32[]{:S(2)}) collective-permute-start(bf16[64,1536]{1,0:T(8,128)(2,1)S(1)} %collective-permute-done.refs_0_.refs_4_), channel_id=1, source_target_pairs={{0,8},{4,12},{8,0},{12,4},{16,24},{20,28},{24,16},{28,20},{1,9},{5... | collective-permute-start | bytes 589832 | tf_op jit(solution)/shard_map/ppermute | solution.py:461
  58.4 86.7 %all-gather.8.cloned.1.call-start = ((), (), s32[]{:S(2)}) async-start(), calls=%async_computation.2 | async-start | bytes 2621440 | tf_op jit(solution)/shard_map/all_gather | solution.py:509
  58.7 4.1 %collective-permute-start.4 = (bf16[64,1536]{1,0:T(8,128)(2,1)S(1)}, bf16[64,1536]{1,0:T(8,128)(2,1)S(1)}, u32[]{:S(2)}, u32[]{:S(2)}) collective-permute-start(bf16[64,1536]{1,0:T(8,128)(2,1)S(1)} %collective-permute-done.3.refs_2_.refs_6_), channel_id=1, source_target_pairs={{0,4},{4,0},{8,12},{12,8},{16,20},{20,16},{24,28},{28,24},{1,5},{5... | collective-permute-start | bytes 589832 | tf_op jit(solution)/shard_map/ppermute | solution.py:465
  59.3 14.5 %collective-permute-start.7 = (bf16[64,2048]{1,0:T(8,128)(2,1)}, bf16[64,2048]{1,0:T(8,128)(2,1)S(1)}, u32[]{:S(2)}, u32[]{:S(2)}) collective-permute-start(bf16[64,2048]{1,0:T(8,128)(2,1)} %get-tuple-element.61), channel_id=1, source_target_pairs={{0,1},{1,0},{2,3},{3,2},{4,5},{5,4},{6,7},{7,6},{8,9},{9,8},{10,11... | collective-permute-start | bytes 786440 | tf_op jit(solution)/shard_map/ppermute | solution.py:457
  60.7 14.2 %collective-permute-start.8 = (bf16[64,2048]{1,0:T(8,128)(2,1)}, bf16[64,2048]{1,0:T(8,128)(2,1)}, u32[]{:S(2)}, u32[]{:S(2)}) collective-permute-start(bf16[64,2048]{1,0:T(8,128)(2,1)} %get-tuple-element.62), channel_id=1, source_target_pairs={{0,2},{1,3},{2,0},{3,1},{4,6},{5,7},{6,4},{7,5},{8,10},{9,11},{10,... | collective-permute-start | bytes 786440 | tf_op jit(solution)/shard_map/ppermute | solution.py:457
  62.3 15.7 %collective-permute-start.9 = (bf16[64,2048]{1,0:T(8,128)(2,1)}, bf16[64,2048]{1,0:T(8,128)(2,1)}, u32[]{:S(2)}, u32[]{:S(2)}) collective-permute-start(bf16[64,2048]{1,0:T(8,128)(2,1)} %get-tuple-element.63), channel_id=1, source_target_pairs={{0,3},{1,2},{2,1},{3,0},{4,7},{5,6},{6,5},{7,4},{8,11},{9,10},{10,... | collective-permute-start | bytes 786440 | tf_op jit(solution)/shard_map/ppermute | solution.py:457
  70.7 12.8 %collective-permute-start.10 = (bf16[64,2048]{1,0:T(8,128)(2,1)}, bf16[64,2048]{1,0:T(8,128)(2,1)}, u32[]{:S(2)}, u32[]{:S(2)}) collective-permute-start(bf16[64,2048]{1,0:T(8,128)(2,1)} %get-tuple-element.65), channel_id=1, source_target_pairs={{0,1},{1,0},{2,3},{3,2},{4,5},{5,4},{6,7},{7,6},{8,9},{9,8},{10,11... | collective-permute-start | bytes 786440 | tf_op jit(solution)/shard_map/ppermute | solution.py:457
  72.2 23.0 %collective-permute-start.11 = (bf16[64,2048]{1,0:T(8,128)(2,1)}, bf16[64,2048]{1,0:T(8,128)(2,1)}, u32[]{:S(2)}, u32[]{:S(2)}) collective-permute-start(bf16[64,2048]{1,0:T(8,128)(2,1)} %get-tuple-element.69), channel_id=1, source_target_pairs={{0,2},{1,3},{2,0},{3,1},{4,6},{5,7},{6,4},{7,5},{8,10},{9,11},{10,... | collective-permute-start | bytes 786440 | tf_op jit(solution)/shard_map/ppermute | solution.py:457
  74.5 20.8 %collective-permute-start.12 = (bf16[64,2048]{1,0:T(8,128)(2,1)}, bf16[64,2048]{1,0:T(8,128)(2,1)}, u32[]{:S(2)}, u32[]{:S(2)}) collective-permute-start(bf16[64,2048]{1,0:T(8,128)(2,1)} %get-tuple-element.70), channel_id=1, source_target_pairs={{0,3},{1,2},{2,1},{3,0},{4,7},{5,6},{6,5},{7,4},{8,11},{9,10},{10,... | collective-permute-start | bytes 786440 | tf_op jit(solution)/shard_map/ppermute | solution.py:457
  81.5 19.5 %collective-permute-start.18 = (bf16[64,2048]{1,0:T(8,128)(2,1)S(1)}, bf16[64,2048]{1,0:T(8,128)(2,1)S(1)}, u32[]{:S(2)}, u32[]{:S(2)}) collective-permute-start(bf16[64,2048]{1,0:T(8,128)(2,1)S(1)} %get-tuple-element.64.refs_0_.refs_5_), channel_id=1, source_target_pairs={{0,3},{1,2},{2,1},{3,0},{4,7},{5,6},{6,5},{7,4},{8,11},{9,10},{10,... | collective-permute-start | bytes 786440 | tf_op jit(solution)/shard_map/ppermute | solution.py:457
  81.8 20.6 %collective-permute-start.17 = (bf16[64,2048]{1,0:T(8,128)(2,1)S(1)}, bf16[64,2048]{1,0:T(8,128)(2,1)S(1)}, u32[]{:S(2)}, u32[]{:S(2)}) collective-permute-start(bf16[64,2048]{1,0:T(8,128)(2,1)S(1)} %get-tuple-element.64.refs_0_.refs_5_), channel_id=1, source_target_pairs={{0,2},{1,3},{2,0},{3,1},{4,6},{5,7},{6,4},{7,5},{8,10},{9,11},{10,... | collective-permute-start | bytes 786440 | tf_op jit(solution)/shard_map/ppermute | solution.py:457
  83.5 18.9 %collective-permute-start.16 = (bf16[64,2048]{1,0:T(8,128)(2,1)S(1)}, bf16[64,2048]{1,0:T(8,128)(2,1)S(1)}, u32[]{:S(2)}, u32[]{:S(2)}) collective-permute-start(bf16[64,2048]{1,0:T(8,128)(2,1)S(1)} %get-tuple-element.64.refs_0_.refs_5_), channel_id=1, source_target_pairs={{0,1},{1,0},{2,3},{3,2},{4,5},{5,4},{6,7},{7,6},{8,9},{9,8},{10,11... | collective-permute-start | bytes 786440 | tf_op jit(solution)/shard_map/ppermute | solution.py:457
  97.8 12.7 %collective-permute-start.15 = (bf16[64,2048]{1,0:T(8,128)(2,1)S(1)}, bf16[64,2048]{1,0:T(8,128)(2,1)S(1)}, u32[]{:S(2)}, u32[]{:S(2)}) collective-permute-start(bf16[64,2048]{1,0:T(8,128)(2,1)S(1)} %get-tuple-element.72.refs_0_.refs_1_), channel_id=1, source_target_pairs={{0,3},{1,2},{2,1},{3,0},{4,7},{5,6},{6,5},{7,4},{8,11},{9,10},{10,... | collective-permute-start | bytes 786440 | tf_op jit(solution)/shard_map/ppermute | solution.py:457
  98.5 13.0 %collective-permute-start.14 = (bf16[64,2048]{1,0:T(8,128)(2,1)S(1)}, bf16[64,2048]{1,0:T(8,128)(2,1)S(1)}, u32[]{:S(2)}, u32[]{:S(2)}) collective-permute-start(bf16[64,2048]{1,0:T(8,128)(2,1)S(1)} %get-tuple-element.72.refs_0_.refs_1_), channel_id=1, source_target_pairs={{0,2},{1,3},{2,0},{3,1},{4,6},{5,7},{6,4},{7,5},{8,10},{9,11},{10,... | collective-permute-start | bytes 786440 | tf_op jit(solution)/shard_map/ppermute | solution.py:457
  100.9 10.5 %collective-permute-start.13 = (bf16[64,2048]{1,0:T(8,128)(2,1)S(1)}, bf16[64,2048]{1,0:T(8,128)(2,1)S(1)}, u32[]{:S(2)}, u32[]{:S(2)}) collective-permute-start(bf16[64,2048]{1,0:T(8,128)(2,1)S(1)} %get-tuple-element.72.refs_0_.refs_1_), channel_id=1, source_target_pairs={{0,1},{1,0},{2,3},{3,2},{4,5},{5,4},{6,7},{7,6},{8,9},{9,8},{10,11... | collective-permute-start | bytes 786440 | tf_op jit(solution)/shard_map/ppermute | solution.py:457
  110.4 8.4 %collective-permute-start.19 = (bf16[4,64,2048]{2,1,0:T(8,128)(2,1)}, bf16[4,64,2048]{2,1,0:T(8,128)(2,1)S(1)}, u32[]{:S(2)}, u32[]{:S(2)}) collective-permute-start(bf16[4,64,2048]{2,1,0:T(8,128)(2,1)} %copy-done.22), channel_id=1, source_target_pairs={{0,4},{4,0},{8,12},{12,8},{16,20},{20,16},{24,28},{28,24},{1,5},{5... | collective-permute-start | bytes 3145736 | tf_op jit(solution)/shard_map/ppermute | solution.py:465
  120.3 23.9 %collective-permute-start.20 = (bf16[64,2048]{1,0:T(8,128)(2,1)S(1)}, bf16[64,2048]{1,0:T(8,128)(2,1)S(1)}, u32[]{:S(2)}, u32[]{:S(2)}) collective-permute-start(bf16[64,2048]{1,0:T(8,128)(2,1)S(1)} %get-tuple-element.80), channel_id=1, source_target_pairs={{0,8},{4,12},{8,0},{12,4},{16,24},{20,28},{24,16},{28,20},{1,9},{5... | collective-permute-start | bytes 786440 | tf_op jit(solution)/shard_map/ppermute | solution.py:461
  121.8 22.4 %collective-permute-start.21 = (bf16[64,2048]{1,0:T(8,128)(2,1)S(1)}, bf16[64,2048]{1,0:T(8,128)(2,1)S(1)}, u32[]{:S(2)}, u32[]{:S(2)}) collective-permute-start(bf16[64,2048]{1,0:T(8,128)(2,1)S(1)} %get-tuple-element.81), channel_id=1, source_target_pairs={{0,16},{4,20},{8,24},{12,28},{16,0},{20,4},{24,8},{28,12},{1,17},{... | collective-permute-start | bytes 786440 | tf_op jit(solution)/shard_map/ppermute | solution.py:461
  124.2 20.0 %collective-permute-start.22 = (bf16[64,2048]{1,0:T(8,128)(2,1)S(1)}, bf16[64,2048]{1,0:T(8,128)(2,1)S(1)}, u32[]{:S(2)}, u32[]{:S(2)}) collective-permute-start(bf16[64,2048]{1,0:T(8,128)(2,1)S(1)} %get-tuple-element.82), channel_id=1, source_target_pairs={{0,24},{4,28},{8,16},{12,20},{16,8},{20,12},{24,0},{28,4},{1,25},{... | collective-permute-start | bytes 786440 | tf_op jit(solution)/shard_map/ppermute | solution.py:461
  (26 other events, 440.3 us)
Sparse Core Ops, SparseCore 0:
  29.3 39.5 all-gather.3
  70.6 30.3 all-gather.5
  110.5 33.9 all-gather.7
